TPU v7x, 512 devices: a whole 4x8x8 slice. The times are simulated.
512 devices in a mesh: tp: 32 (over z, y_hi), ep: 16 (over y_lo, x, core).
Axes of the slice: x: 4, y: 8 (y_hi: 4, y_lo: 2; y = y_hi * 2 + y_lo), z: 8, core: 2. Of those that a mesh axis runs over, the one named last changes fastest.
Arguments:
- tokens: bfloat16 [16, 96, 7168], P('ep', 'tp'), may hold values from -6 to 6
- gain: float32 [7168], replicated, may hold values from 0.25 to 1.75
- routes: int32 [16, 96, 2], P('ep', 'tp'), may hold values from 0 to 15, all different within a row; in each aligned block of 96 rows (0 to 95, 96 to 191, ..., all dimensions but the last counted through in order) at most 18 rows name the same one
- gate_frac: int32 [16, 96, 2], P('ep', 'tp'), may hold values from 1 to 255
- dense_gate: bfloat16 [7168, 4864], P('ep', 'tp'), may hold values from -0.0625 to 0.0625
- dense_up: bfloat16 [7168, 4864], P('ep', 'tp'), may hold values from -0.0625 to 0.0625
- dense_down: bfloat16 [4864, 7168], P('tp', 'ep'), may hold values from -0.15625 to 0.15625
- expert_gate: bfloat16 [16, 7168, 2432], P('ep', 'tp'), may hold values from -0.0625 to 0.0625
- expert_up: bfloat16 [16, 7168, 2432], P('ep', 'tp'), may hold values from -0.0625 to 0.0625
- expert_down: bfloat16 [16, 2432, 7168], P('ep', None, 'tp'), may hold values from -0.125 to 0.125
Outputs:
- mixed: bfloat16 [16, 96, 7168], P('ep', None, 'tp')
Inputs may be any that keep to these rules, and one draw needn't show every extreme that they name: `routes`: the two experts of a token differ. Among the 96 tokens of one index of the first dimension no expert is named more than 18 times, and in every draw some expert is named exactly 18 times by some such group. A route's weight is gate_frac / 256.
All inputs are finite; a program needn't handle non-finite values.
Results may differ from a plain program's by a relative error of at most 0.033.
Values may be sent and summed in bfloat16 or wider, within the bound.
No kernel may reach another device: no remote copies, remote signals or barrier semaphores. Data moves between devices by JAX's collectives and lax.ppermute only.
A program may use at most 64 MiB of HBM per device.

v0:
```python
import jax
import jax.numpy as jnp
from jax import lax
from jax.sharding import PartitionSpec as P

D = 7168


EPS = 1e-05


def rms_norm(rows, gain):
    values = rows.astype(jnp.float32)
    scale = lax.rsqrt(jnp.mean(values * values, axis=-1, keepdims=True) + EPS)
    return (values * scale * gain).astype(jnp.bfloat16)


def rounded_term(values):
    return lax.optimization_barrier(values.astype(jnp.bfloat16)).astype(jnp.float32)


def swish_product(gate_pre, up_pre):
    return (jax.nn.silu(gate_pre) * up_pre).astype(jnp.bfloat16)


def local(
    tokens,
    gain,
    routes,
    gate_frac,
    dense_gate,
    dense_up,
    dense_down,
    expert_gate,
    expert_up,
    expert_down,
):
    tp_count = lax.axis_size("tp")
    ep_count = lax.axis_size("ep")
    normed = rms_norm(tokens[0], gain)
    gathered, route_ids, fractions = (
        lax.all_gather(normed, "tp", axis=0, tiled=True),
        lax.all_gather(routes[0], "tp", axis=0, tiled=True),
        lax.all_gather(gate_frac[0], "tp", axis=0, tiled=True),
    )
    group_rows = gathered.shape[0]
    capacity = 3 * group_rows // ep_count
    slot_count = ep_count * capacity
    slice_width = D // tp_count
    flat_ids = route_ids.reshape(-1)
    expert_hot = (flat_ids[:, None] == jnp.arange(ep_count, dtype=jnp.int32)[None, :]).astype(
        jnp.int32
    )
    earlier = jnp.cumsum(expert_hot, axis=0) - expert_hot
    position = jnp.sum(earlier * expert_hot, axis=1)
    slot_index = flat_ids * capacity + position
    slot_hot = (slot_index[:, None] == jnp.arange(slot_count, dtype=jnp.int32)[None, :]).astype(
        jnp.float32
    )
    route_weight = fractions.reshape(-1).astype(jnp.float32) / 256.0
    dispatch_table = slot_hot.reshape(group_rows, 2, slot_count).sum(axis=1).astype(jnp.bfloat16)
    combine_table = (
        (slot_hot * route_weight[:, None])
        .reshape(group_rows, 2, slot_count)
        .sum(axis=1)
        .astype(jnp.bfloat16)
    )
    own_columns = lax.dynamic_slice_in_dim(
        gathered, lax.axis_index("tp") * slice_width, slice_width, 1
    )
    first = jnp.dot(
        gathered,
        lax.all_gather(dense_gate, "ep", axis=0, tiled=True),
        preferred_element_type=jnp.float32,
    )
    second = jnp.dot(
        gathered,
        lax.all_gather(dense_up, "ep", axis=0, tiled=True),
        preferred_element_type=jnp.float32,
    )
    dense_hidden = swish_product(first, second)
    partial_value = jnp.dot(
        dense_hidden,
        lax.all_gather(dense_down, "ep", axis=1, tiled=True),
        preferred_element_type=jnp.float32,
    ).astype(jnp.bfloat16)
    dense_out = lax.psum_scatter(
        partial_value.astype(jnp.float32).astype(jnp.bfloat16),
        "tp",
        scatter_dimension=1,
        tiled=True,
    ).astype(jnp.float32)
    outgoing = jnp.einsum(
        "rs,rd->sd", dispatch_table, own_columns, preferred_element_type=jnp.float32
    ).astype(jnp.bfloat16)
    arrived = lax.all_to_all(outgoing, "ep", split_axis=0, concat_axis=0, tiled=True)
    gate_term = rounded_term(jnp.dot(arrived, expert_gate[0], preferred_element_type=jnp.float32))
    up_term = rounded_term(jnp.dot(arrived, expert_up[0], preferred_element_type=jnp.float32))
    gate_share, up_share = (
        lax.psum_scatter(
            gate_term.astype(jnp.bfloat16), "tp", scatter_dimension=0, tiled=True
        ).astype(jnp.float32),
        lax.psum_scatter(
            up_term.astype(jnp.bfloat16), "tp", scatter_dimension=0, tiled=True
        ).astype(jnp.float32),
    )
    expert_hidden = lax.all_gather(swish_product(gate_share, up_share), "tp", axis=0, tiled=True)
    expert_result = jnp.dot(
        expert_hidden, expert_down[0], preferred_element_type=jnp.float32
    ).astype(jnp.bfloat16)
    returned = lax.all_to_all(expert_result, "ep", split_axis=0, concat_axis=0, tiled=True)
    moe_out = jnp.dot(combine_table, returned, preferred_element_type=jnp.float32)
    return (dense_out + moe_out).astype(jnp.bfloat16)[None]


def solution(mesh):
    placed = (
        P("ep", "tp", None),
        P(),
        P("ep", "tp", None),
        P("ep", "tp", None),
        P("ep", "tp"),
        P("ep", "tp"),
        P("tp", "ep"),
        P("ep", "tp", None),
        P("ep", "tp", None),
        P("ep", None, "tp"),
    )
    return jax.shard_map(
        local, mesh=mesh, in_specs=placed, out_specs=P("ep", None, "tp"), check_vma=False
    )
```

profile of v0, /device:TPU:6, one launch (start us, length us, event | category | flops | bytes accessed | tf_op | source)
XLA Modules:
  0.0 799.9 jit_solution(45133033871305873)
XLA Ops:
  7.4 1.1 fusion.11
  8.5 1.5 fusion.22
  10.1 0.8 copy.31
  10.8 88.4 %all-gather = s32[1,96,2]{2,0,1:T(1,128)S(1)} all-gather(s32[1,3,2]{2,0,1:T(1,128)S(1)} %copy.31), channel_id=2, replica_groups=mesh['tp'=32,'ep'=16] {'tp'}, dimensions={1}, use_global_device_ids=true | all-gather | bytes 792 | tf_op jit(solution)/shard_map/all_gather | solution.py:43
  99.7 0.8 reduce.5
  100.7 0.6 reduce-window.6
  101.8 0.8 copy.36
  102.6 75.5 %all-gather.1 = s32[1,96,2]{2,0,1:T(1,128)S(1)} all-gather(s32[1,3,2]{2,0,1:T(1,128)S(1)} %copy.36), channel_id=3, replica_groups=mesh['tp'=32,'ep'=16] {'tp'}, dimensions={1}, use_global_device_ids=true | all-gather | bytes 792 | tf_op jit(solution)/shard_map/all_gather | solution.py:44
  178.4 3.0 reshape.78
  181.7 11.9 %all_to_all.24 = bf16[16,18,224]{2,1,0:T(8,128)(2,1)S(1)} all-to-all(bf16[16,18,224]{2,1,0:T(8,128)(2,1)S(1)} %all_to_all.16), channel_id=1, replica_groups=mesh['tp'=32,'ep'=16] {'ep'}, dimensions={0} | all-to-all | bytes 258048 | tf_op jit(solution)/shard_map/all_to_all | solution.py:96
  193.7 1.7 convolution_convert_fusion.2
  195.3 1.6 convolution_convert_fusion.1
  198.8 1.3 dynamic-slice
  200.7 324.9 %all-reduce.6.cloned.1.call-done = (bf16[288,2432]{1,0:T(8,128)(2,1)}, bf16[288,2432]{1,0:T(8,128)(2,1)}) async-done(((bf16[288,2432]{1,0:T(8,128)(2,1)}, bf16[288,2432]{1,0:T(8,128)(2,1)}), (bf16[288,2432]{1,0:T(8,128)(2,1)}, bf16[288,2432]{1,0:T(8,128)(2,1)})) %all-reduce.6.cloned.1.call-update) | async-done | bytes 2801680
  525.6 1.7 fusion.19
  527.6 3.9 copy.28
  531.5 5.1 reshape.80
  536.7 4.0 copy.29
  540.7 5.1 reshape.82
  545.8 4.0 copy.30
  549.7 5.1 reshape.84
  554.9 2.4 fusion.29
  557.3 5.4 convolution_convert_fusion
  562.7 3.6 copy.38
  566.3 45.9 %all-gather.21.cloned.1.call-done = bf16[32,9,2432]{2,1,0:T(8,128)(2,1)} async-done(((bf16[1,9,2432]{2,1,0:T(8,128)(2,1)}), bf16[32,9,2432]{2,1,0:T(8,128)(2,1)}) %all-gather.21.cloned.1.call-update) | async-done | bytes 1400848 | tf_op jit(solution)/shard_map/all_gather | solution.py:107
  612.2 2.0 reshape.86
  614.2 1.8 convolution_convert_fusion.3
  616.0 0.7 all_to_all.19
  616.7 4.8 all-to-all-start.1
  621.6 169.2 %reduce-scatter.4.cloned.1.call-done = bf16[224,96]{1,0:T(8,128)(2,1)} async-done(((bf16[7168,96]{1,0:T(8,128)(2,1)}), bf16[224,96]{1,0:T(8,128)(2,1)}) %reduce-scatter.4.cloned.1.call-update) | async-done | bytes 43024
  790.8 0.9 copy.39
  791.8 0.8 fusion.2
  (43 shorter events, 4.1 us)
Async XLA Ops:
  7.4 186.3 %copy-start = (bf16[1,224,2432]{2,1,0:T(8,128)(2,1)S(1)}, bf16[1,224,2432]{2,1,0:T(8,128)(2,1)}, u32[]{:S(2)}) copy-start(bf16[1,224,2432]{2,1,0:T(8,128)(2,1)} %param.17) | copy-start | bytes 3268612
  7.4 171.0 %all-gather.13.cloned.1.call-start = ((), (), s32[]{:S(2)}) async-start(), calls=%async_computation.3 | async-start | bytes 1892352 | tf_op jit(solution)/shard_map/all_gather | solution.py:42
  10.0 515.6 %all-reduce.6.cloned.1.call-start = ((), (), s32[]{:S(2)}) async-start(), calls=%async_computation.9 | async-start | bytes 5603328
  193.6 1.7 copy-start.1
  197.0 330.6 %all-gather.15.cloned.1.call-start = ((), (), s32[]{:S(2)}) async-start(), calls=%async_computation.4 | async-start | bytes 2646016 | tf_op jit(solution)/shard_map/all_gather | solution.py:73
  197.6 339.1 %all-gather.17.cloned.1.call-start = ((), (), s32[]{:S(2)}) async-start(), calls=%async_computation.5 | async-start | bytes 2646016 | tf_op jit(solution)/shard_map/all_gather | solution.py:78
  198.2 347.6 %all-gather.19.cloned.1.call-start = ((), (), s32[]{:S(2)}) async-start(), calls=%async_computation.6 | async-start | bytes 2646016 | tf_op jit(solution)/shard_map/all_gather | solution.py:84
  198.7 413.4 %all-gather.21.cloned.1.call-start = ((), (), s32[]{:S(2)}) async-start(), calls=%async_computation.7 | async-start | bytes 2568192 | tf_op jit(solution)/shard_map/all_gather | solution.py:107
  527.3 263.5 %reduce-scatter.4.cloned.1.call-start = ((), (), s32[]{:S(2)}) async-start(), calls=%async_computation.8 | async-start | bytes 1892352
  616.7 175.0 %all-to-all-start.1 = ((bf16[16,18,224]{2,1,0:T(8,128)(2,1)}), bf16[16,18,224]{2,1,0:T(8,128)(2,1)S(1)}, u32[]{:S(2)}, u32[]{:S(2)}) async-start(bf16[16,18,224]{2,1,0:T(8,128)(2,1)} %all_to_all.19), calls=%async_computation.1 | async-start | bytes 393216 | tf_op jit(solution)/shard_map/all_to_all | solution.py:111
Sparse Core Ops, SparseCore 0:
  11.4 89.4 all-gather.12
  197.1 328.4 all-reduce.5
  566.4 224.2 reduce-scatter.3
Sparse Core Ops, SparseCore 1:
  199.6 33.7 all-gather.14
  235.4 42.5 all-gather.16
  279.9 41.3 all-gather.18
  527.4 84.7 all-gather.20
where the time goes:
time: 801 us; the launch traced here: 800 us
  waiting for transfers between devices  542 us (68%)
  blocking collectives  176 us (22%)
  local copies, waits for them, and re-layouts  41.7 us (5%)
  between operations  15.6 us (2%)
  matrix products  14 us (2%)
    unnamed x9, waiting for transfers between devices  496 us
    all_gather x1, blocking collectives, local(): lax.all_gather(routes[0], 'tp', axis=0, tiled=True)  88.4 us
    all_gather x1, blocking collectives, local(): lax.all_gather(gate_frac[0], 'tp', axis=0, tiled=True)  75.5 us
    all_gather x1, waiting for transfers between devices, local(): lax.all_gather(swish_product(gate_share, up_share), 'tp', axis=0, tiled=T...  45.9 us
    unnamed x14, local copies, waits for them, and re-layouts  27.7 us
  transfers between devices with their start and end apart: 8, of which 3 were waited for; matrix products, arithmetic and copies ran while one was open for 6% of the time, Pallas kernels for 0%

commit v1 on v0

--- a/solution.py
+++ b/solution.py
@@ -15,12 +15,18 @@
     return (values * scale * gain).astype(jnp.bfloat16)
 
 
-def rounded_term(values):
-    return lax.optimization_barrier(values.astype(jnp.bfloat16)).astype(jnp.float32)
+def swish_product(gate_pre, up_pre):
+    return (jax.nn.silu(gate_pre) * up_pre).astype(jnp.bfloat16)
 
 
-def swish_product(gate_pre, up_pre):
-    return (jax.nn.silu(gate_pre) * up_pre).astype(jnp.bfloat16)
+def share(block, axis):
+    copies = jnp.broadcast_to(block[None], (lax.axis_size(axis), *block.shape))
+    return lax.all_to_all(lax.optimization_barrier(copies), axis, 0, 0, tiled=True)
+
+
+def exchange_sum(blocks, axis):
+    moved = lax.all_to_all(blocks, axis, 0, 0, tiled=True)
+    return jnp.sum(moved.astype(jnp.float32), axis=0)
 
 
 def local(
@@ -38,11 +44,12 @@
     tp_count = lax.axis_size("tp")
     ep_count = lax.axis_size("ep")
     normed = rms_norm(tokens[0], gain)
-    gathered, route_ids, fractions = (
-        lax.all_gather(normed, "tp", axis=0, tiled=True),
-        lax.all_gather(routes[0], "tp", axis=0, tiled=True),
-        lax.all_gather(gate_frac[0], "tp", axis=0, tiled=True),
-    )
+    small = jnp.concatenate([routes[0], gate_frac[0]], axis=1).astype(jnp.bfloat16)
+    row = jnp.concatenate([normed, jnp.pad(small, ((0, 0), (0, 124)))], axis=1)
+    arrived_rows = share(row, "tp").reshape(-1, D + 128)
+    gathered = arrived_rows[:, :D]
+    route_ids = arrived_rows[:, D : D + 2].astype(jnp.int32)
+    fractions = arrived_rows[:, D + 2 : D + 4].astype(jnp.int32)
     group_rows = gathered.shape[0]
     capacity = 3 * group_rows // ep_count
     slot_count = ep_count * capacity
@@ -84,31 +91,32 @@
         lax.all_gather(dense_down, "ep", axis=1, tiled=True),
         preferred_element_type=jnp.float32,
     ).astype(jnp.bfloat16)
-    dense_out = lax.psum_scatter(
-        partial_value.astype(jnp.float32).astype(jnp.bfloat16),
-        "tp",
-        scatter_dimension=1,
-        tiled=True,
-    ).astype(jnp.float32)
+    dense_out = exchange_sum(
+        partial_value.reshape(group_rows, tp_count, slice_width).transpose(1, 0, 2), "tp"
+    )
     outgoing = jnp.einsum(
         "rs,rd->sd", dispatch_table, own_columns, preferred_element_type=jnp.float32
     ).astype(jnp.bfloat16)
-    arrived = lax.all_to_all(outgoing, "ep", split_axis=0, concat_axis=0, tiled=True)
-    gate_term = rounded_term(jnp.dot(arrived, expert_gate[0], preferred_element_type=jnp.float32))
-    up_term = rounded_term(jnp.dot(arrived, expert_up[0], preferred_element_type=jnp.float32))
-    gate_share, up_share = (
-        lax.psum_scatter(
-            gate_term.astype(jnp.bfloat16), "tp", scatter_dimension=0, tiled=True
-        ).astype(jnp.float32),
-        lax.psum_scatter(
-            up_term.astype(jnp.bfloat16), "tp", scatter_dimension=0, tiled=True
-        ).astype(jnp.float32),
+    arrived = lax.all_to_all(
+        outgoing.reshape(ep_count, capacity, -1), "ep", split_axis=0, concat_axis=0, tiled=True
+    ).reshape(slot_count, -1)
+    terms = jnp.stack(
+        [
+            jnp.dot(arrived, expert_gate[0], preferred_element_type=jnp.float32),
+            jnp.dot(arrived, expert_up[0], preferred_element_type=jnp.float32),
+        ]
+    ).astype(jnp.bfloat16)
+    per_device = slot_count // tp_count
+    gate_share, up_share = exchange_sum(
+        terms.reshape(2, tp_count, per_device, -1).transpose(1, 0, 2, 3), "tp"
     )
-    expert_hidden = lax.all_gather(swish_product(gate_share, up_share), "tp", axis=0, tiled=True)
+    expert_hidden = share(swish_product(gate_share, up_share), "tp").reshape(slot_count, -1)
     expert_result = jnp.dot(
         expert_hidden, expert_down[0], preferred_element_type=jnp.float32
     ).astype(jnp.bfloat16)
-    returned = lax.all_to_all(expert_result, "ep", split_axis=0, concat_axis=0, tiled=True)
+    returned = lax.all_to_all(
+        expert_result.reshape(ep_count, capacity, -1), "ep", split_axis=0, concat_axis=0, tiled=True
+    ).reshape(slot_count, -1)
     moe_out = jnp.dot(combine_table, returned, preferred_element_type=jnp.float32)
     return (dense_out + moe_out).astype(jnp.bfloat16)[None]
 

time: 801 us -> 372 us (0.46)
  waiting for transfers between devices: 542 us -> 219 us
  blocking collectives: 176 us -> 10.9 us
  starting transfers between devices: 5.24 us -> 50.8 us
  local copies, waits for them, and re-layouts: 41.7 us -> 50.9 us
    unnamed x9 -> x3, waiting for transfers between devices: 496 us -> 2.06 us
    all_to_all x1 -> x5, waiting for transfers between devices: 0.01 us -> 211 us  [the longest x2 128 us: exchange_sum(): moved = lax.all_to_all(blocks, axis, 0, 0, tiled=True)]
    all_gather x2 -> x0, blocking collectives: 164 us -> none  [the longest x1 88.4 us: local(): lax.all_gather(routes[0], 'tp', axis=0, tiled=True)]
    all_to_all x1 -> x5, starting transfers between devices: 4.81 us -> 50.7 us  [the longest x2 25.1 us: share(): lax.all_to_all(lax.optimization_barrier(copies), axis, 0, 0, tiled=True)]
    all_gather x2 -> x0, waiting for transfers between devices: 45.9 us -> none  [the longest x1 45.9 us: local(): lax.all_gather(swish_product(gate_share, up_share), 'tp', axis=0, tiled=T...]
    reshape x0 -> x7, local copies, waits for them, and re-layouts: none -> 13.6 us  [the longest x2 7.79 us: local(): partial_value.reshape(group_rows, tp_count, slice_width).transpose(1, 0, 2)]
    unnamed x14 -> x10, local copies, waits for them, and re-layouts: 27.7 us -> 16.3 us
  transfers between devices with their start and end apart: 8 -> 8, of which waited for: 3 -> 6; matrix products, arithmetic and copies ran while one was open for 6% -> 18% of each run, Pallas kernels for 0% -> 0%
where the time goes in v1:
time: 372 us; the launch traced here: 368 us
  waiting for transfers between devices  219 us (59%)
  local copies, waits for them, and re-layouts  50.9 us (14%)
  starting transfers between devices  50.8 us (14%)
  between operations  13.3 us (4%)
  matrix products  12.6 us (3%)
  blocking collectives  10.9 us (3%)
  other arithmetic  10.1 us (3%)
    all_to_all x2, waiting for transfers between devices, exchange_sum(): moved = lax.all_to_all(blocks, axis, 0, 0, tiled=True)  128 us
    all_to_all x2, waiting for transfers between devices, share(): lax.all_to_all(lax.optimization_barrier(copies), axis, 0, 0, tiled=True)  79.6 us
    all_to_all x2, starting transfers between devices, share(): lax.all_to_all(lax.optimization_barrier(copies), axis, 0, 0, tiled=True)  25.1 us
    all_to_all x2, starting transfers between devices, exchange_sum(): moved = lax.all_to_all(blocks, axis, 0, 0, tiled=True)  21.1 us
    unnamed x10, local copies, waits for them, and re-layouts  16.3 us
    all_to_all x1, blocking collectives, local(): lax.all_to_all(outgoing.reshape(ep_count, capacity, -1), 'ep', split_axis...  10.9 us
    reshape x2, local copies, waits for them, and re-layouts, local(): partial_value.reshape(group_rows, tp_count, slice_width).transpose(1, 0, 2)  7.79 us
  transfers between devices with their start and end apart: 8, of which 6 were waited for; matrix products, arithmetic and copies ran while one was open for 18% of the time, Pallas kernels for 0%

profile of v1, /device:TPU:6, one launch (start us, length us, event | category | flops | bytes accessed | tf_op | source)
XLA Modules:
  0.0 367.7 jit_solution(5223615612562543051)
XLA Ops:
  9.4 1.7 broadcast_in_dim.8
  11.1 16.1 %all-to-all-start = ((bf16[32,3,7296]{2,1,0:T(4,128)(2,1)}), bf16[32,3,7296]{2,1,0:T(4,128)(2,1)}, u32[]{:S(2)}, u32[]{:S(2)}) async-start(bf16[32,3,7296]{2,1,0:T(4,128)(2,1)} %broadcast_in_dim.8), calls=%async_computation | async-start | bytes 3735552 | tf_op jit(solution)/shard_map/all_to_all | solution.py:24
  28.0 56.7 %all-to-all-done = bf16[32,3,7296]{2,1,0:T(4,128)(2,1)} async-done(((bf16[32,3,7296]{2,1,0:T(4,128)(2,1)}), bf16[32,3,7296]{2,1,0:T(4,128)(2,1)}, u32[]{:S(2)}, u32[]{:S(2)}) %all-to-all-start) | async-done | bytes 1400864 | tf_op jit(solution)/shard_map/all_to_all | solution.py:24
  84.7 3.0 reshape.100
  87.7 1.2 slice.24
  90.5 1.1 convolution_convert_fusion.4
  91.8 10.9 %all_to_all.30 = bf16[16,18,224]{2,1,0:T(8,128)(2,1)S(1)} all-to-all(bf16[16,18,224]{2,1,0:T(8,128)(2,1)S(1)} %reshape.104), channel_id=1, replica_groups=mesh['tp'=32,'ep'=16] {'ep'}, dimensions={0} | all-to-all | bytes 258048 | tf_op jit(solution)/shard_map/all_to_all | solution.py:100
  104.8 3.7 %copy.83 = bf16[32,2,9,2432]{3,1,2,0:T(2,128)(2,1)} copy(bf16[32,2,9,2432]{3,0,2,1:T(8,128)(2,1)S(1)} %maximum_bitcast_fusion) | data formatting | bytes 5603328 | tf_op jit(solution)/shard_map/transpose | solution.py:111
  108.5 10.9 %all-to-all-start.3 = ((bf16[32,2,9,2432]{3,1,2,0:T(2,128)(2,1)}), bf16[32,2,9,2432]{3,1,2,0:T(2,128)(2,1)}, u32[]{:S(2)}, u32[]{:S(2)}) async-start(bf16[32,2,9,2432]{3,1,2,0:T(2,128)(2,1)} %copy.83), calls=%async_computation.3 | async-start | bytes 5603328 | tf_op jit(solution)/shard_map/all_to_all | solution.py:28
  120.9 86.4 %all-to-all-done.3 = bf16[32,2,9,2432]{3,1,2,0:T(2,128)(2,1)} async-done(((bf16[32,2,9,2432]{3,1,2,0:T(2,128)(2,1)}), bf16[32,2,9,2432]{3,1,2,0:T(2,128)(2,1)}, u32[]{:S(2)}, u32[]{:S(2)}) %all-to-all-start.3) | async-done | bytes 2801696 | tf_op jit(solution)/shard_map/all_to_all | solution.py:28
  207.2 4.2 %convert_reduce_fusion = f32[2,9,2432]{2,0,1:T(2,128)S(1)} fusion(bf16[32,2,9,2432]{3,1,2,0:T(2,128)(2,1)} %all-to-all-done.3), kind=kLoop, calls=%fused_computation.1 | loop fusion | flops 2757888 | bytes 2976768 | tf_op jit(solution)/shard_map/reduce_sum | solution.py:29
  211.6 1.6 broadcast_in_dim.10
  213.3 9.0 %all-to-all-start.4 = ((bf16[32,9,2432]{2,1,0:T(8,128)(2,1)}), bf16[32,9,2432]{2,1,0:T(8,128)(2,1)}, u32[]{:S(2)}, u32[]{:S(2)}) async-start(bf16[32,9,2432]{2,1,0:T(8,128)(2,1)} %broadcast_in_dim.10), calls=%async_computation.4 | async-start | bytes 4980736 | tf_op jit(solution)/shard_map/all_to_all | solution.py:24
  222.4 4.0 %copy.73 = bf16[16,448,152]{1,0,2:T(8,128)(2,1)} copy(bf16[16,448,152]{1,2,0:T(8,128)(2,1)} %all-gather.7.cloned.1.call-done) | data formatting | bytes 4358144 | tf_op jit(solution)/shard_map/all_gather | solution.py:80
  226.4 5.1 %reshape.112 = bf16[7168,152]{0,1:T(8,128)(2,1)} reshape(bf16[16,448,152]{1,0,2:T(8,128)(2,1)} %copy.73) | data formatting | bytes 4358144
  231.5 4.0 %copy.74 = bf16[16,448,152]{1,0,2:T(8,128)(2,1)} copy(bf16[16,448,152]{1,2,0:T(8,128)(2,1)} %all-gather.9.cloned.1.call-done) | data formatting | bytes 4358144 | tf_op jit(solution)/shard_map/all_gather | solution.py:85
  235.5 5.1 %reshape.114 = bf16[7168,152]{0,1:T(8,128)(2,1)} reshape(bf16[16,448,152]{1,0,2:T(8,128)(2,1)} %copy.74) | data formatting | bytes 4358144
  240.6 5.9 %all-gather.11.cloned.1.call-done = bf16[16,448,152]{1,2,0:T(8,128)(2,1)} async-done(((bf16[1,448,152]{1,2,0:T(8,128)(2,1)}), bf16[16,448,152]{1,2,0:T(8,128)(2,1)}) %all-gather.11.cloned.1.call-update) | async-done | bytes 2179088 | tf_op jit(solution)/shard_map/all_gather | solution.py:91
  246.5 4.0 %copy.75 = bf16[16,448,152]{1,0,2:T(8,128)(2,1)} copy(bf16[16,448,152]{1,2,0:T(8,128)(2,1)} %all-gather.11.cloned.1.call-done) | data formatting | bytes 4358144 | tf_op jit(solution)/shard_map/all_gather | solution.py:91
  250.6 5.2 %reshape.116 = bf16[7168,152]{0,1:T(8,128)(2,1)} reshape(bf16[16,448,152]{1,0,2:T(8,128)(2,1)} %copy.75) | data formatting | bytes 4358144
  255.7 2.4 fusion.32
  258.1 5.3 %convolution_convert_fusion = bf16[96,7168]{1,0:T(8,128)(2,1)} fusion(bf16[7168,152]{0,1:T(8,128)(2,1)} %reshape.116, bf16[7168,152]{0,1:T(8,128)(2,1)} %reshape.114, f32[96,152]{0,1:T(8,128)S(1)} %fusion.32, bf16[96,7296]{1,0:T(8,128)(2,1)S(1)} %reshape.100), kind=kOutput, calls=%fused_computation | convolution fusion | flops 419157504 | bytes 7188480 | tf_op jit(solution)/shard_map/dot_general | solution.py:89
  263.5 4.3 %reshape.101 = bf16[96,32,224]{2,1,0:T(8,128)(2,1)} reshape(bf16[96,7168]{1,0:T(8,128)(2,1)} %convolution_convert_fusion) | data formatting | bytes 2752512 | tf_op jit(solution)/shard_map/reshape | solution.py:95
  267.8 3.5 copy.97
  271.2 22.9 %all-to-all-done.4 = bf16[32,9,2432]{2,1,0:T(8,128)(2,1)} async-done(((bf16[32,9,2432]{2,1,0:T(8,128)(2,1)}), bf16[32,9,2432]{2,1,0:T(8,128)(2,1)}, u32[]{:S(2)}, u32[]{:S(2)}) %all-to-all-start.4) | async-done | bytes 1400864 | tf_op jit(solution)/shard_map/all_to_all | solution.py:24
  294.2 10.2 %all-to-all-start.1 = ((bf16[32,96,224]{2,1,0:T(8,128)(2,1)}), bf16[32,96,224]{2,1,0:T(8,128)(2,1)}, u32[]{:S(2)}, u32[]{:S(2)}) async-start(bf16[32,96,224]{2,1,0:T(8,128)(2,1)} %bitcast.63), calls=%async_computation.1 | async-start | bytes 3145728 | tf_op jit(solution)/shard_map/all_to_all | solution.py:28
  304.4 2.0 reshape.106
  306.4 1.8 convolution_convert_fusion.3
  308.9 41.7 %all-to-all-done.1 = bf16[32,96,224]{2,1,0:T(8,128)(2,1)} async-done(((bf16[32,96,224]{2,1,0:T(8,128)(2,1)}), bf16[32,96,224]{2,1,0:T(8,128)(2,1)}, u32[]{:S(2)}, u32[]{:S(2)}) %all-to-all-start.1) | async-done | bytes 1376288 | tf_op jit(solution)/shard_map/all_to_all | solution.py:28
  350.6 4.5 %all-to-all-start.5 = ((bf16[16,18,224]{2,1,0:T(8,128)(2,1)}), bf16[16,18,224]{2,1,0:T(8,128)(2,1)S(1)}, u32[]{:S(2)}, u32[]{:S(2)}) async-start(bf16[16,18,224]{2,1,0:T(8,128)(2,1)} %reshape.107), calls=%async_computation.5 | async-start | bytes 393216 | tf_op jit(solution)/shard_map/all_to_all | solution.py:117
  355.1 1.7 convert_reduce_fusion.1
  356.8 3.5 all-to-all-done.5
  (45 shorter events, 10.7 us)
Async XLA Ops:
  6.5 96.1 %copy-start = (bf16[1,224,2432]{2,1,0:T(8,128)(2,1)S(1)}, bf16[1,224,2432]{2,1,0:T(8,128)(2,1)}, u32[]{:S(2)}) copy-start(bf16[1,224,2432]{2,1,0:T(8,128)(2,1)} %param.17) | copy-start | bytes 3268612
  11.1 73.5 %all-to-all-start = ((bf16[32,3,7296]{2,1,0:T(4,128)(2,1)}), bf16[32,3,7296]{2,1,0:T(4,128)(2,1)}, u32[]{:S(2)}, u32[]{:S(2)}) async-start(bf16[32,3,7296]{2,1,0:T(4,128)(2,1)} %broadcast_in_dim.8), calls=%async_computation | async-start | bytes 3735552 | tf_op jit(solution)/shard_map/all_to_all | solution.py:24
  27.2 195.1 %all-gather.7.cloned.1.call-start = ((), (), s32[]{:S(2)}) async-start(), calls=%async_computation.6 | async-start | bytes 2646016 | tf_op jit(solution)/shard_map/all_gather | solution.py:80
  102.7 1.2 copy-start.1
  108.5 98.8 %all-to-all-start.3 = ((bf16[32,2,9,2432]{3,1,2,0:T(2,128)(2,1)}), bf16[32,2,9,2432]{3,1,2,0:T(2,128)(2,1)}, u32[]{:S(2)}, u32[]{:S(2)}) async-start(bf16[32,2,9,2432]{3,1,2,0:T(2,128)(2,1)} %copy.83), calls=%async_computation.3 | async-start | bytes 5603328 | tf_op jit(solution)/shard_map/all_to_all | solution.py:28
  119.4 112.1 %all-gather.9.cloned.1.call-start = ((), (), s32[]{:S(2)}) async-start(), calls=%async_computation.7 | async-start | bytes 2646016 | tf_op jit(solution)/shard_map/all_gather | solution.py:85
  120.1 126.4 %all-gather.11.cloned.1.call-start = ((), (), s32[]{:S(2)}) async-start(), calls=%async_computation.8 | async-start | bytes 2646016 | tf_op jit(solution)/shard_map/all_gather | solution.py:91
  213.3 80.9 %all-to-all-start.4 = ((bf16[32,9,2432]{2,1,0:T(8,128)(2,1)}), bf16[32,9,2432]{2,1,0:T(8,128)(2,1)}, u32[]{:S(2)}, u32[]{:S(2)}) async-start(bf16[32,9,2432]{2,1,0:T(8,128)(2,1)} %broadcast_in_dim.10), calls=%async_computation.4 | async-start | bytes 4980736 | tf_op jit(solution)/shard_map/all_to_all | solution.py:24
  294.2 56.4 %all-to-all-start.1 = ((bf16[32,96,224]{2,1,0:T(8,128)(2,1)}), bf16[32,96,224]{2,1,0:T(8,128)(2,1)}, u32[]{:S(2)}, u32[]{:S(2)}) async-start(bf16[32,96,224]{2,1,0:T(8,128)(2,1)} %bitcast.63), calls=%async_computation.1 | async-start | bytes 3145728 | tf_op jit(solution)/shard_map/all_to_all | solution.py:28
  350.6 9.7 %all-to-all-start.5 = ((bf16[16,18,224]{2,1,0:T(8,128)(2,1)}), bf16[16,18,224]{2,1,0:T(8,128)(2,1)S(1)}, u32[]{:S(2)}, u32[]{:S(2)}) async-start(bf16[16,18,224]{2,1,0:T(8,128)(2,1)} %reshape.107), calls=%async_computation.5 | async-start | bytes 393216 | tf_op jit(solution)/shard_map/all_to_all | solution.py:117
Sparse Core Ops, SparseCore 0:
  30.2 54.3 all-gather.6
  122.4 64.1 all-gather.8
  188.8 57.7 all-gather.10

commit v2 on v0

v2 whole, which is shorter than its diff:
```python
import jax
import jax.numpy as jnp
import numpy as np
from jax import lax
from jax.experimental import pallas as pl
from jax.experimental.pallas import tpu as pltpu
from jax.sharding import Mesh, PartitionSpec as P

D = 7168
EPS = 1e-05
Z, YH, YL, X, C = 8, 4, 2, 4, 2
EP = YL * X * C
TP = Z * YH
ROWS = 96
CAP = 18
LAND = 24
SLOT = 20
EFF = 2432
HID = 640
FEAT = 224
HALF = 448
WIDE = 1024
BLOCK = 160
SHARE = 2 * BLOCK
MATES = 4
MOE_Z = EP * SLOT // Z
DENSE_Z = MATES * ROWS // Z // 2
ROW_Z = MOE_Z + DENSE_Z
BF, F32 = jnp.bfloat16, jnp.float32


def call(kernel, outs, args, scalars=(), scratch=(), flops=0):
    specs = [pl.BlockSpec(memory_space=pltpu.SMEM)] * len(scalars)
    specs += [pl.BlockSpec(memory_space=pltpu.VMEM)] * len(args)
    moved = sum(a.size * a.dtype.itemsize for a in args)
    moved += sum(o.size * o.dtype.itemsize for o in outs)
    single = len(outs) == 1
    return pl.pallas_call(
        kernel,
        out_shape=outs[0] if single else outs,
        in_specs=specs,
        out_specs=pl.BlockSpec(memory_space=pltpu.VMEM)
        if single
        else [pl.BlockSpec(memory_space=pltpu.VMEM)] * len(outs),
        scratch_shapes=list(scratch),
        compiler_params=pltpu.CompilerParams(vmem_limit_bytes=40 * 1024 * 1024),
        cost_estimate=pl.CostEstimate(flops=flops, bytes_accessed=moved, transcendentals=0),
    )(*scalars, *args)


def struct(shape, dtype=BF):
    return jax.ShapeDtypeStruct(shape, dtype)


def iota(shape, dim):
    return lax.broadcasted_iota(jnp.int32, shape, dim)


def dot(a, b):
    return jnp.dot(a, b, preferred_element_type=F32)


def rms_norm(rows, gain):
    values = rows.astype(F32)
    scale = lax.rsqrt(jnp.mean(values * values, axis=-1, keepdims=True) + EPS)
    return (values * scale * gain).astype(BF)


def dispatch_kernel(got, tokens_out, slots_out, mix_out):
    token, row = iota((ROWS, 4 * TP), 0), iota((ROWS, 4 * TP), 1)
    pick = (token == 3 * (row >> 2) + (row & 3)) & ((row & 3) < 3)
    tokens = dot(pick.astype(F32).astype(BF), got[...]).astype(BF)
    tokens_out[...] = tokens
    meta = jnp.transpose(tokens[:, 384:512].astype(F32), (1, 0))
    first, second = meta[64:65, :], meta[65:66, :]
    expert = iota((EP, ROWS), 0).astype(F32)
    hot_a = (expert == first).astype(F32)
    hot_b = (expert == second).astype(F32)
    earlier = (iota((ROWS, ROWS), 0) < iota((ROWS, ROWS), 1)).astype(F32).astype(BF)
    count = dot((hot_a + hot_b).astype(BF), earlier)
    slot_a = first * LAND + jnp.sum(hot_a * count, axis=0, keepdims=True)
    slot_b = second * LAND + jnp.sum(hot_b * count, axis=0, keepdims=True)
    slot = iota((EP * LAND, ROWS), 0).astype(F32)
    at_a, at_b = (slot == slot_a).astype(F32), (slot == slot_b).astype(F32)
    slots_out[...] = dot((at_a + at_b).astype(BF), tokens).astype(BF)
    mix = (at_a * meta[66:67, :] + at_b * meta[67:68, :]) * (1.0 / 256.0)
    mix_out[...] = jnp.transpose(mix, (1, 0)).astype(BF)


def assemble_kernel(me, part0, part1, part2, part3, gate_out, up_out):
    for out in (gate_out, up_out):
        for half in range(2):
            out[512 * half + HALF : 512 * (half + 1), :] = jnp.zeros((64, HID), BF)
    for k, part in enumerate((part0, part1, part2, part3)):
        source = me[0] ^ k
        start = pl.multiple_of((source >> 1) * 512 + (source & 1) * FEAT, 16)
        gate_out[pl.ds(start, FEAT), :] = part[0:FEAT, :]
        up_out[pl.ds(start, FEAT), :] = part[FEAT : 2 * FEAT, :]


def dense_up_kernel(column, mate, rows, weights, out, held):
    lane = iota((BLOCK, 128), 1)

    def put(branch, first, half, width, values):
        for low, high, place in ((0, 256, 256 * branch), (256, SHARE, 512 + 64 * branch)):
            begin, end = max(first, low), min(first + BLOCK, high)
            if begin < end:
                held[place + begin - low : place + end - low, half : half + width] = values[
                    begin - first : end - first, :
                ]

    for half in range(2):
        for q in range(2):
            part = weights.at[(2 * half + q) ^ column[0]]
            tail = part[:, 768:896].astype(F32)
            tails = (tail, pltpu.roll(tail, 64, 1))
            for branch in range(2):
                put(branch, q * BLOCK, 512 * half, 384, part[:, 384 * branch : 384 * (branch + 1)])
                last = jnp.where(lane < 64, tails[branch], 0.0).astype(BF)
                put(branch, q * BLOCK, 512 * half + 384, 128, last)
    for i in range(MATES):
        out[ROWS * i : ROWS * (i + 1), :] = lax.dot_general(
            rows[mate[0] ^ i], held[...], (((1,), (1,)), ((), ())), preferred_element_type=F32
        ).astype(BF)


def expert_up_kernel(got, gate, up, dense, out):
    row, column = iota((EP * SLOT, EP * LAND), 0), iota((EP * SLOT, EP * LAND), 1)
    group = ((row.astype(F32) + 0.5) * (1.0 / SLOT)).astype(jnp.int32)
    place = row - SLOT * group
    pick = (column == LAND * group + place) & (place < CAP)
    rows = dot(pick.astype(F32).astype(BF), got[...]).astype(BF)
    for branch, weights in enumerate((gate, up)):
        pre = dot(rows, weights[...])
        other = dense[...].astype(F32)
        for z in range(Z):
            out[z, :, HID * branch : HID * (branch + 1)] = jnp.concatenate(
                [
                    pre[MOE_Z * z : MOE_Z * (z + 1)],
                    other[DENSE_Z * (2 * z + branch) : DENSE_Z * (2 * z + branch + 1)],
                ],
                axis=0,
            ).astype(BF)


def swish(gate, up):
    return gate / (1.0 + jnp.exp(-gate)) * up


def hidden_kernel(me, got, out):
    total = got[0].astype(F32)
    for z in range(1, Z):
        total = total + got[z].astype(F32)
    expert = swish(total[:MOE_Z, :HID], total[:MOE_Z, HID:])
    twice = iota((MOE_Z, HID), 1) < YH * HID - EFF
    expert = jnp.where(twice & (me[0] == YH - 1), 0.0, expert)
    pieces, tails = [], []
    for half in range(2):
        rows = total[MOE_Z:, HID * half : HID * (half + 1)]
        pieces.append(swish(rows[:, :256], rows[:, 256:512]))
        tail = rows[:, 512:640]
        tails.append(swish(tail, pltpu.roll(tail, 64, 1)))
    lane = iota((DENSE_Z, 128), 1)
    pieces.append(jnp.where(lane < 64, tails[0], pltpu.roll(tails[1], 64, 1)))
    hidden = jnp.concatenate([expert, jnp.concatenate(pieces, axis=1)], axis=0).astype(BF)
    for z in range(Z):
        out[z] = hidden


def dense_down_kernel(column, got, dense, own_out, *outs_and_held):
    *others, held = outs_and_held
    held[...] = jnp.zeros(held.shape, BF)
    for half in range(2):
        for side in range(2):
            for q in range(2):
                values = dense.at[(2 * half + q) ^ column[0]]
                first, left = q * BLOCK, 896 + 256 * side
                for low, high, step, place in ((0, 256, 256, 0), (256, SHARE, 64, 512)):
                    begin, end = max(first, low), min(first + BLOCK, high)
                    if begin < end:
                        for i in range(2):
                            at = place + step * i
                            held[2 * half + side, i, at + begin - low : at + end - low, :] = values[
                                begin - first : end - first, left : left + FEAT
                            ]
    rows = got[...].astype(F32)
    rows = jnp.concatenate(
        [rows[ROW_Z * z + MOE_Z : ROW_Z * (z + 1)] for z in range(Z)], axis=0
    ).astype(BF)
    for target in range(YH):
        sums = [dot(rows, held[target, i]) for i in range(2)]
        for mate, out in enumerate((own_out, *others)):
            pieces = []
            for z in (2 * mate, 2 * mate + 1):
                pieces += [part[DENSE_Z * z : DENSE_Z * (z + 1)] for part in sums]
            out[target] = jnp.concatenate(pieces, axis=0).astype(out.dtype)


def expert_down_kernel(me, got, part0, part1, part2, part3, out):
    rows = got[...].astype(F32)
    rows = jnp.concatenate(
        [rows[ROW_Z * z : ROW_Z * z + MOE_Z] for z in range(Z)], axis=0
    ).astype(BF)
    for k, part in enumerate((part0, part1, part2, part3)):
        out[me[0] ^ k] = lax.dot_general(
            rows, part[...], (((1,), (1,)), ((), ())), preferred_element_type=F32
        ).astype(BF)


def result_kernel(got, slots_out, own_out):
    total = got[0].astype(F32)
    for k in range(1, YH):
        total = total + got[k].astype(F32)
    expert = total[: EP * SLOT]
    slot, row = iota((EP * LAND, EP * SLOT), 0), iota((EP * LAND, EP * SLOT), 1)
    group = ((slot.astype(F32) + 0.5) * (1.0 / LAND)).astype(jnp.int32)
    place = slot - LAND * group
    pick = (row == SLOT * group + place) & (place < CAP)
    slots_out[...] = dot(pick.astype(F32).astype(BF), expert.astype(BF)).astype(BF)
    own_out[...] = total[EP * SLOT :]


def turn_pairs():
    return [
        (z * EP + i, z * EP + ((i // C + z) % (YL * X)) * C + i % C)
        for z in range(Z)
        for i in range(EP)
    ]


def spread_pairs():
    pairs = []
    for z in range(Z):
        for i in range(EP):
            x, yl, c = (i % 2) * 2 + z % 2, z // 4, z // 2 % 2
            pairs.append((z * EP + i, (i // 2) * EP + yl * X * C + x * C + c))
    turned = dict(turn_pairs())
    return [(turned[source], target) for source, target in pairs]


SWAP = [(0, 1), (1, 0)]
CROSS = [(0, 3), (1, 2), (2, 1), (3, 0)]


def to_mates(first, second, third):
    return (
        lax.ppermute(first, "c", SWAP),
        lax.ppermute(second, "yl", SWAP),
        lax.ppermute(third, ("yl", "c"), CROSS),
    )


def local(
    tokens,
    gain,
    routes,
    gate_frac,
    dense_gate,
    dense_up,
    dense_down,
    expert_gate,
    expert_up,
    expert_down,
):
    position = lax.axis_index("yh")
    me = position.astype(jnp.int32).reshape(1)

    normed = rms_norm(tokens[0], gain)
    parts = jnp.pad(normed.reshape(3, Z, 2, HALF), ((0, 0), (0, 0), (0, 0), (0, 64)))
    small = jnp.concatenate([routes[0], gate_frac[0]], axis=1).astype(BF)
    small = jnp.pad(small, ((0, 0), (HALF, 60)))
    parts = parts + jnp.stack([small, jnp.zeros_like(small)], axis=1)[:, None]
    parts = jnp.pad(parts.reshape(3, Z, WIDE).transpose(1, 0, 2), ((0, 0), (0, 1), (0, 0)))
    send = jnp.broadcast_to(parts[:, None], (Z, YH, 4, WIDE)).reshape(TP, 4, WIDE)
    ups, downs = [], []
    for k in range(YH):
        start = HID * (position ^ k)
        ups.append(
            jnp.concatenate(
                [
                    lax.dynamic_slice_in_dim(expert_gate[0], start, HID, 1),
                    lax.dynamic_slice_in_dim(expert_up[0], start, HID, 1),
                ]
            )
        )
        downs.append(lax.dynamic_slice_in_dim(expert_down[0].T, start, HID, 1))

    def moved(block, k):
        return lax.ppermute(block, "yh", [(i, i ^ k) for i in range(YH)])

    for k in (1, 3):
        ups[k] = moved(ups[k], k)

    def padded(block):
        return jnp.pad(block, ((0, BLOCK - 152), (0, 0)))

    plane = ("z", "yl", "x", "c")
    gate_in, up_in, low = padded(dense_gate.T), padded(dense_up.T), padded(dense_down)
    dense = [gate_in[:, :384], up_in[:, :384], gate_in[:, 384:], up_in[:, 384:]]
    for side in range(2):
        part = low[:, FEAT * side : FEAT * (side + 1)]
        dense.append(jnp.pad(part, ((0, 0), (0, 256 - FEAT))))
    dense = lax.ppermute(jnp.concatenate(dense, axis=1), plane, turn_pairs())
    dense = lax.ppermute(dense, plane, spread_pairs())
    got = lax.all_to_all(send, ("z", "yh"), 0, 0, tiled=True).reshape(4 * TP, WIDE)
    column = lax.axis_index("x").astype(jnp.int32).reshape(1)
    own, slots, mix = call(
        dispatch_kernel,
        [struct((ROWS, WIDE)), struct((EP * LAND, WIDE)), struct((ROWS, EP * LAND))],
        [got],
        flops=2 * EP * LAND * ROWS * WIDE,
    )
    own, dense = lax.optimization_barrier((own, dense))
    mates = [lax.all_gather(own, ("yl", "c"), axis=0)]
    mate = (2 * lax.axis_index("yl") + lax.axis_index("c")).astype(jnp.int32).reshape(1)
    ups[2] = moved(ups[2], 2)
    dense = jnp.stack(
        [dense]
        + [lax.ppermute(dense, "x", [(i, i ^ k) for i in range(X)]) for k in range(1, X)]
    )
    arrived = lax.all_to_all(
        slots.reshape(EP, LAND, WIDE), ("yl", "x", "c"), 0, 0, tiled=True
    ).reshape(EP * LAND, WIDE)

    gate, up = call(
        assemble_kernel, [struct((WIDE, HID)), struct((WIDE, HID))], ups, scalars=[me]
    )
    gate, up, *mates = lax.optimization_barrier((gate, up, *mates))
    dense_pre = call(
        dense_up_kernel,
        [struct((MATES * ROWS, 2 * SHARE))],
        [*mates, dense],
        scalars=[column, mate],
        scratch=[pltpu.VMEM((2 * SHARE, WIDE), BF)],
        flops=4 * MATES * ROWS * WIDE * SHARE,
    )
    pre = call(
        expert_up_kernel,
        [struct((Z, ROW_Z, 2 * HID))],
        [arrived, gate, up, dense_pre],
        flops=4 * EP * SLOT * WIDE * HID,
    )
    pre, *downs = lax.optimization_barrier((pre, *downs))
    pre = lax.all_to_all(pre, "z", 0, 0, tiled=True)
    hidden = call(hidden_kernel, [struct((Z, ROW_Z, HID))], [pre], scalars=[me])
    downs[1:] = [moved(downs[k], k) for k in range(1, YH)]
    hidden, *downs = lax.optimization_barrier((hidden, *downs))
    hidden = lax.all_to_all(hidden, "z", 0, 0, tiled=True)
    hidden = hidden.reshape(Z * ROW_Z, HID)
    own_sum, *others = call(
        dense_down_kernel,
        [struct((YH, ROWS, FEAT), F32 if i == 0 else BF) for i in range(MATES)],
        [hidden, dense],
        scalars=[column],
        scratch=[pltpu.VMEM((YH, 2, HID, FEAT), BF)],
        flops=16 * MATES * ROWS * HID * FEAT,
    )
    from_mates = to_mates(*others)
    partial = call(
        expert_down_kernel,
        [struct((YH, EP * SLOT, FEAT))],
        [hidden, *downs],
        scalars=[me],
        flops=8 * EP * SLOT * HID * FEAT,
    )
    for sent in from_mates:
        own_sum = own_sum + sent.astype(F32)
    partial = jnp.concatenate([partial, own_sum.astype(BF)], axis=1)
    partial = lax.all_to_all(partial, "yh", 0, 0, tiled=True)
    result, own_sum = call(
        result_kernel,
        [struct((EP * LAND, FEAT)), struct((ROWS, FEAT), F32)],
        [partial],
        flops=2 * EP * LAND * EP * SLOT * FEAT,
    )
    returned = lax.all_to_all(
        result.reshape(EP, LAND, FEAT), ("yl", "x", "c"), 0, 0, tiled=True
    ).reshape(EP * LAND, FEAT)
    return (own_sum + dot(mix, returned)).astype(BF)[None]


def solution(mesh):
    split = Mesh(
        np.asarray(mesh.devices).reshape(Z, YH, YL, X, C), ("z", "yh", "yl", "x", "c")
    )
    tp, ep = ("z", "yh"), ("yl", "x", "c")
    placed = (
        P(ep, tp, None),
        P(),
        P(ep, tp, None),
        P(ep, tp, None),
        P(ep, tp),
        P(ep, tp),
        P(tp, ep),
        P(ep, tp, None),
        P(ep, tp, None),
        P(ep, None, tp),
    )
    return jax.shard_map(
        local, mesh=split, in_specs=placed, out_specs=P(ep, None, tp), check_vma=False
    )
```

time: 801 us -> 265 us (0.33)
  waiting for transfers between devices: 542 us -> 59.7 us
  blocking collectives: 176 us -> 84.5 us
  starting transfers between devices: 5.24 us -> 86.9 us
  local copies, waits for them, and re-layouts: 41.7 us -> 10.9 us
  between operations: 15.6 us -> 0.49 us
  matrix products: 14 us -> 0.8 us
  Pallas kernels: 0 us -> 10.7 us
    unnamed x9 -> x0, waiting for transfers between devices: 496 us -> none
    all_gather x2 -> x1, blocking collectives: 164 us -> 19 us  [local(): mates = [lax.all_gather(own, ('yl', 'c'), axis=0)]]
    ppermute x0 -> x14, starting transfers between devices: none -> 55.6 us  [the longest x6 23 us: moved(): return lax.ppermute(block, 'yh', [(i, i ^ k) for i in range(YH)])]
    all_to_all x1 -> x3, blocking collectives: 11.9 us -> 65.6 us  [the longest x1 26.8 us: local(): partial = lax.all_to_all(partial, 'yh', 0, 0, tiled=True)]
    all_gather x5 -> x0, waiting for transfers between devices: 45.9 us -> none  [the longest x1 45.9 us: local(): lax.all_gather(swish_product(gate_share, up_share), 'tp', axis=0, tiled=T...]
    ppermute x0 -> x14, waiting for transfers between devices: none -> 35.5 us  [the longest x6 20.9 us: moved(): return lax.ppermute(block, 'yh', [(i, i ^ k) for i in range(YH)])]
    all_to_all x1 -> x3, starting transfers between devices: 4.81 us -> 31.3 us  [the longest x1 16.1 us: local(): lax.all_to_all(send, ('z', 'yh'), 0, 0, tiled=True).reshape(4 * TP, WIDE)]
    unnamed x14 -> x30, local copies, waits for them, and re-layouts: 27.7 us -> 2.87 us
  transfers between devices with their start and end apart: 8 -> 17, of which waited for: 3 -> 7; matrix products, arithmetic and copies ran while one was open for 6% -> 4% of each run, Pallas kernels for 0% -> 3%
where the time goes in v2:
time: 265 us; the launch traced here: 261 us
  starting transfers between devices  86.9 us (33%)
  blocking collectives  84.5 us (32%)
  waiting for transfers between devices  59.7 us (23%)
  local copies, waits for them, and re-layouts  10.9 us (4%)
  Pallas kernels  10.7 us (4%)
  other arithmetic  6.55 us (2%)
    all_to_all x1, blocking collectives, local(): partial = lax.all_to_all(partial, 'yh', 0, 0, tiled=True)  26.8 us
    all_to_all x1, blocking collectives, local(): hidden = lax.all_to_all(hidden, 'z', 0, 0, tiled=True)  25.8 us
    ppermute x6, starting transfers between devices, moved(): return lax.ppermute(block, 'yh', [(i, i ^ k) for i in range(YH)])  23 us
    all_to_all x1, waiting for transfers between devices, local(): pre = lax.all_to_all(pre, 'z', 0, 0, tiled=True)  22.6 us
    ppermute x6, waiting for transfers between devices, moved(): return lax.ppermute(block, 'yh', [(i, i ^ k) for i in range(YH)])  20.9 us
    all_gather x1, blocking collectives, local(): mates = [lax.all_gather(own, ('yl', 'c'), axis=0)]  19 us
    all_to_all x1, starting transfers between devices, local(): lax.all_to_all(send, ('z', 'yh'), 0, 0, tiled=True).reshape(4 * TP, WIDE)  16.1 us
    all_to_all x1, blocking collectives, local(): lax.all_to_all(result.reshape(EP, LAND, FEAT), ('yl', 'x', 'c'), 0, 0, ti...  13 us
  transfers between devices with their start and end apart: 17, of which 7 were waited for; matrix products, arithmetic and copies ran while one was open for 4% of the time, Pallas kernels for 3%

profile of v2, /device:TPU:6, one launch (start us, length us, event | category | flops | bytes accessed | tf_op | source)
XLA Modules:
  0.0 260.6 jit_solution(8327393639576117996)
XLA Ops:
  4.9 16.1 %all-to-all-start = ((bf16[32,4,1024]{2,1,0:T(4,128)(2,1)}), bf16[32,4,1024]{2,1,0:T(4,128)(2,1)}, u32[]{:S(2)}, u32[]{:S(2)}) async-start(bf16[32,4,1024]{2,1,0:T(4,128)(2,1)} %bitcast.5), calls=%async_computation | async-start | bytes 524288 | tf_op jit(solution)/shard_map/all_to_all | solution.py:305
  22.1 5.1 %collective-permute-start.3 = (bf16[160,1408]{1,0:T(8,128)(2,1)}, bf16[160,1408]{1,0:T(8,128)(2,1)}, u32[]{:S(2)}, u32[]{:S(2)}) collective-permute-start(bf16[160,1408]{1,0:T(8,128)(2,1)} %concatenate.27), channel_id=1, source_target_pairs={{0,0},{1,1},{2,2},{3,3},{4,4},{5,5},{6,6},{7,7},{8,8},{9,9},{10,10... | collective-permute-start | bytes 1351688 | tf_op jit(solution)/shard_map/ppermute | solution.py:303
  29.2 4.7 %collective-permute-start = (bf16[448,640]{1,0:T(8,128)(2,1)}, bf16[448,640]{1,0:T(8,128)(2,1)S(1)}, u32[]{:S(2)}, u32[]{:S(2)}) collective-permute-start(bf16[448,640]{1,0:T(8,128)(2,1)} %pad_maximum_fusion.3), channel_id=1, source_target_pairs={{0,16},{16,0},{32,48},{48,32},{1,17},{17,1},{33,49},{49,33},{2,18}... | collective-permute-start | bytes 1720328 | tf_op jit(solution)/shard_map/ppermute | solution.py:289
  38.0 4.9 %all-to-all-start.1 = ((bf16[16,24,1024]{2,1,0:T(8,128)(2,1)}), bf16[16,24,1024]{2,1,0:T(8,128)(2,1)S(1)}, u32[]{:S(2)}, u32[]{:S(2)}) async-start(bf16[16,24,1024]{2,1,0:T(8,128)(2,1)} %bitcast.6), calls=%async_computation.1 | async-start | bytes 1572864 | tf_op jit(solution)/shard_map/all_to_all | solution.py:321
  42.9 9.6 %collective-permute-start.4 = (bf16[160,1408]{1,0:T(8,128)(2,1)}, bf16[160,1408]{1,0:T(8,128)(2,1)}, u32[]{:S(2)}, u32[]{:S(2)}) collective-permute-start(bf16[160,1408]{1,0:T(8,128)(2,1)} %collective-permute-done.3), channel_id=1, source_target_pairs={{0,0},{1,4},{2,64},{3,68},{4,128},{5,132},{6,192},{7,196},{8,256},... | collective-permute-start | bytes 1351688 | tf_op jit(solution)/shard_map/ppermute | solution.py:304
  53.5 4.2 %collective-permute-start.1 = (bf16[448,640]{1,0:T(8,128)(2,1)}, bf16[448,640]{1,0:T(8,128)(2,1)S(1)}, u32[]{:S(2)}, u32[]{:S(2)}) collective-permute-start(bf16[448,640]{1,0:T(8,128)(2,1)} %pad_maximum_fusion.4), channel_id=1, source_target_pairs={{0,32},{16,48},{32,0},{48,16},{1,33},{17,49},{33,1},{49,17},{2,34}... | collective-permute-start | bytes 1720328 | tf_op jit(solution)/shard_map/ppermute | solution.py:289
  58.6 1.9 collective-permute-start.2
  60.5 9.1 %collective-permute-done.4 = bf16[160,1408]{1,0:T(8,128)(2,1)} collective-permute-done((bf16[160,1408]{1,0:T(8,128)(2,1)}, bf16[160,1408]{1,0:T(8,128)(2,1)}, u32[]{:S(2)}, u32[]{:S(2)}) %collective-permute-start.4) | collective-permute-done | bytes 450592 | tf_op jit(solution)/shard_map/ppermute | solution.py:304
  69.6 1.9 collective-permute-start.5
  71.6 1.9 collective-permute-start.6
  73.5 6.6 %collective-permute-start.7 = (bf16[160,1408]{1,0:T(8,128)(2,1)}, bf16[160,1408]{1,0:T(8,128)(2,1)}, u32[]{:S(2)}, u32[]{:S(2)}) collective-permute-start(bf16[160,1408]{1,0:T(8,128)(2,1)} %collective-permute-done.4), channel_id=1, source_target_pairs={{0,6},{2,4},{4,2},{6,0},{1,7},{3,5},{5,3},{7,1},{8,14},{10,12},{12... | collective-permute-start | bytes 1351688 | tf_op jit(solution)/shard_map/ppermute | solution.py:319
  80.2 2.2 dynamic-slice_bitcast_fusion
  82.3 11.5 %collective-permute-done.1.part2 = bf16[448,640]{1,0:T(8,128)(2,1)S(1)} collective-permute-done((bf16[448,640]{1,0:T(8,128)(2,1)}, bf16[448,640]{1,0:T(8,128)(2,1)S(1)}, u32[]{:S(2)}, u32[]{:S(2)}) %collective-permute-start.1) | collective-permute-done | bytes 573472 | tf_op jit(solution)/shard_map/ppermute | solution.py:289
  93.8 9.4 %collective-permute-done.2.part3 = bf16[448,640]{1,0:T(8,128)(2,1)} collective-permute-done((bf16[448,640]{1,0:T(8,128)(2,1)}, bf16[448,640]{1,0:T(8,128)(2,1)}, u32[]{:S(2)}, u32[]{:S(2)}) %collective-permute-start.2) | collective-permute-done | bytes 573472 | tf_op jit(solution)/shard_map/ppermute | solution.py:289
  104.5 19.0 %all-gather = bf16[384,1024]{1,0:T(8,128)(2,1)S(1)} all-gather(bf16[96,1024]{1,0:T(8,128)(2,1)S(1)} %get-tuple-element.35), channel_id=2, replica_groups=mesh['z'=8,'yh'=4,'yl'=2,'x'=4,'c'=2] {'yl','c'}, dimensions={0}, use_global_device_ids=true | all-gather | bytes 983040 | tf_op jit(solution)/shard_map/all_gather | solution.py:314
  123.5 1.7 pad_maximum_fusion.weights.dense
  125.2 1.7 shard_map.102.dense
  129.6 2.6 %shard_map.103 = bf16[8,64,1280]{2,1,0:T(8,128)(2,1)} custom-call(bf16[384,1024]{1,0:T(8,128)(2,1)S(1)} %bitcast.59, bf16[1024,640]{1,0:T(8,128)(2,1)S(1)} %copy-done.1, bf16[1024,640]{1,0:T(8,128)(2,1)S(1)} %copy-done.3, bf16[384,640]{1,0:T(8,128)(2,1)S(1)} %shard_map.102.dense), custom_call_target="tpu_custom_call" | custom-call | flops 838860800 | bytes 5210112 | tf_op jit(solution)/shard_map/pallas_call | solution.py:38
  132.3 10.2 %all-to-all-start.2 = ((bf16[8,64,1280]{2,1,0:T(8,128)(2,1)}), bf16[8,64,1280]{2,1,0:T(8,128)(2,1)S(1)}, u32[]{:S(2)}, u32[]{:S(2)}) async-start(bf16[8,64,1280]{2,1,0:T(8,128)(2,1)} %shard_map.103), calls=%async_computation.2 | async-start | bytes 2621440 | tf_op jit(solution)/shard_map/all_to_all | solution.py:344
  142.5 1.9 collective-permute-start.10
  144.4 4.4 %collective-permute-start.8 = (bf16[224,640]{1,0:T(8,128)(2,1)}, bf16[224,640]{1,0:T(8,128)(2,1)}, u32[]{:S(2)}, u32[]{:S(2)}) collective-permute-start(bf16[224,640]{1,0:T(8,128)(2,1)} %get-tuple-element.42), channel_id=1, source_target_pairs={{0,16},{16,0},{32,48},{48,32},{1,17},{17,1},{33,49},{49,33},{2,18}... | collective-permute-start | bytes 860168 | tf_op jit(solution)/shard_map/ppermute | solution.py:289
  148.9 5.9 %collective-permute-start.9 = (bf16[224,640]{1,0:T(8,128)(2,1)}, bf16[224,640]{1,0:T(8,128)(2,1)}, u32[]{:S(2)}, u32[]{:S(2)}) collective-permute-start(bf16[224,640]{1,0:T(8,128)(2,1)} %get-tuple-element.43), channel_id=1, source_target_pairs={{0,32},{16,48},{32,0},{48,16},{1,33},{17,49},{33,1},{49,17},{2,34}... | collective-permute-start | bytes 860168 | tf_op jit(solution)/shard_map/ppermute | solution.py:289
  154.7 22.6 %all-to-all-done.2.got = bf16[8,64,1280]{2,1,0:T(8,128)(2,1)S(1)} async-done(((bf16[8,64,1280]{2,1,0:T(8,128)(2,1)}), bf16[8,64,1280]{2,1,0:T(8,128)(2,1)S(1)}, u32[]{:S(2)}, u32[]{:S(2)}) %all-to-all-start.2) | async-done | bytes 1310752 | tf_op jit(solution)/shard_map/all_to_all | solution.py:344
  177.8 25.8 %all_to_all.30 = bf16[8,64,640]{2,1,0:T(8,128)(2,1)S(1)} all-to-all(bf16[8,64,640]{2,1,0:T(8,128)(2,1)S(1)} %shard_map.104), channel_id=1, replica_groups=mesh['z'=8,'yh'=4,'yl'=2,'x'=4,'c'=2] {'z'}, dimensions={0} | all-to-all | bytes 1310720 | tf_op jit(solution)/shard_map/all_to_all | solution.py:348
  204.6 1.9 collective-permute-start.11
  206.5 1.9 collective-permute-start.12
  208.4 3.7 %collective-permute-start.13 = (bf16[4,96,224]{2,1,0:T(8,128)(2,1)S(1)}, bf16[4,96,224]{2,1,0:T(8,128)(2,1)S(1)}, u32[]{:S(2)}, u32[]{:S(2)}) collective-permute-start(bf16[4,96,224]{2,1,0:T(8,128)(2,1)S(1)} %get-tuple-element.53), channel_id=1, source_target_pairs={{0,9},{1,8},{8,1},{9,0},{2,11},{3,10},{10,3},{11,2},{4,13},{5,12},... | collective-permute-start | bytes 516104 | tf_op jit(solution)/shard_map/ppermute | solution.py:249
  212.2 1.8 shard_map.105
  214.0 2.1 collective-permute-done.12
  216.1 3.4 %collective-permute-done.13 = bf16[4,96,224]{2,1,0:T(8,128)(2,1)S(1)} collective-permute-done((bf16[4,96,224]{2,1,0:T(8,128)(2,1)S(1)}, bf16[4,96,224]{2,1,0:T(8,128)(2,1)S(1)}, u32[]{:S(2)}, u32[]{:S(2)}) %collective-permute-start.13) | collective-permute-done | bytes 172064 | tf_op jit(solution)/shard_map/ppermute | solution.py:249
  219.7 26.8 %all_to_all.31.got = bf16[4,416,224]{2,1,0:T(8,128)(2,1)S(1)} all-to-all(bf16[4,416,224]{2,1,0:T(8,128)(2,1)S(1)} %pad_maximum_fusion.1), channel_id=1, replica_groups=mesh['z'=8,'yh'=4,'yl'=2,'x'=4,'c'=2] {'yh'}, dimensions={0} | all-to-all | bytes 1490944 | tf_op jit(solution)/shard_map/all_to_all | solution.py:369
  246.9 13.0 %all_to_all.32 = bf16[16,24,224]{2,1,0:T(8,128)(2,1)S(1)} all-to-all(bf16[16,24,224]{2,1,0:T(8,128)(2,1)S(1)} %bitcast.63), channel_id=1, replica_groups=mesh['z'=8,'yh'=4,'yl'=2,'x'=4,'c'=2] {'yl','x','c'}, dimensions={0} | all-to-all | bytes 344064 | tf_op jit(solution)/shard_map/all_to_all | solution.py:376
  (73 shorter events, 20.5 us)
Async XLA Ops:
  0.0 21.0 %copy-start.12 = (bf16[152,448]{1,0:T(8,128)(2,1)S(1)}, bf16[152,448]{1,0:T(8,128)(2,1)}, u32[]{:S(2)}) copy-start(bf16[152,448]{1,0:T(8,128)(2,1)} %param.16) | copy-start | bytes 408580
  1.0 20.1 %copy-start.13 = (pred[256]{0:T(512)(128)(4,1)S(1)}, pred[256]{0:T(512)(128)(4,1)}, u32[]{:S(2)}) copy-start(pred[256]{0:T(512)(128)(4,1)} %constant.49.clone.1) | copy-start | bytes 772
  2.7 18.4 %copy-start.10 = (bf16[448,152]{0,1:T(8,128)(2,1)S(1)}, bf16[448,152]{0,1:T(8,128)(2,1)}, u32[]{:S(2)}) copy-start(bf16[448,152]{0,1:T(8,128)(2,1)} %param.15) | copy-start | bytes 408580
  2.7 18.4 %copy-start.11 = (bf16[448,152]{0,1:T(8,128)(2,1)S(1)}, bf16[448,152]{0,1:T(8,128)(2,1)}, u32[]{:S(2)}) copy-start(bf16[448,152]{0,1:T(8,128)(2,1)} %param.14) | copy-start | bytes 408580
  4.9 30.5 %all-to-all-start = ((bf16[32,4,1024]{2,1,0:T(4,128)(2,1)}), bf16[32,4,1024]{2,1,0:T(4,128)(2,1)}, u32[]{:S(2)}, u32[]{:S(2)}) async-start(bf16[32,4,1024]{2,1,0:T(4,128)(2,1)} %bitcast.5), calls=%async_computation | async-start | bytes 524288 | tf_op jit(solution)/shard_map/all_to_all | solution.py:305
  21.1 6.1 %copy-start.4 = (bf16[1,224,2432]{2,1,0:T(8,128)(2,1)S(1)}, bf16[1,224,2432]{2,1,0:T(8,128)(2,1)}, u32[]{:S(2)}) copy-start(bf16[1,224,2432]{2,1,0:T(8,128)(2,1)} %param.18) | copy-start | bytes 3268612
  21.1 6.1 %copy-start.5 = (bf16[1,224,2432]{2,1,0:T(8,128)(2,1)S(1)}, bf16[1,224,2432]{2,1,0:T(8,128)(2,1)}, u32[]{:S(2)}) copy-start(bf16[1,224,2432]{2,1,0:T(8,128)(2,1)} %param.17) | copy-start | bytes 3268612
  22.1 20.8 %collective-permute-start.3 = (bf16[160,1408]{1,0:T(8,128)(2,1)}, bf16[160,1408]{1,0:T(8,128)(2,1)}, u32[]{:S(2)}, u32[]{:S(2)}) collective-permute-start(bf16[160,1408]{1,0:T(8,128)(2,1)} %concatenate.27), channel_id=1, source_target_pairs={{0,0},{1,1},{2,2},{3,3},{4,4},{5,5},{6,6},{7,7},{8,8},{9,9},{10,10... | collective-permute-start | bytes 1351688 | tf_op jit(solution)/shard_map/ppermute | solution.py:303
  29.2 23.3 %copy-start.8 = (bf16[224,640]{1,0:T(8,128)(2,1)S(1)}, bf16[224,640]{1,0:T(8,128)(2,1)}, u32[]{:S(2)}) copy-start(bf16[224,640]{1,0:T(8,128)(2,1)} %get-tuple-element.68) | copy-start | bytes 860164
  29.2 23.4 %copy-start.9 = (bf16[224,640]{1,0:T(8,128)(2,1)S(1)}, bf16[224,640]{1,0:T(8,128)(2,1)}, u32[]{:S(2)}) copy-start(bf16[224,640]{1,0:T(8,128)(2,1)} %get-tuple-element.71) | copy-start | bytes 860164
  29.2 44.3 %collective-permute-start = (bf16[448,640]{1,0:T(8,128)(2,1)}, bf16[448,640]{1,0:T(8,128)(2,1)S(1)}, u32[]{:S(2)}, u32[]{:S(2)}) collective-permute-start(bf16[448,640]{1,0:T(8,128)(2,1)} %pad_maximum_fusion.3), channel_id=1, source_target_pairs={{0,16},{16,0},{32,48},{48,32},{1,17},{17,1},{33,49},{49,33},{2,18}... | collective-permute-start | bytes 1720328 | tf_op jit(solution)/shard_map/ppermute | solution.py:289
  38.0 19.7 %copy-start.6 = (bf16[224,640]{1,0:T(8,128)(2,1)S(1)}, bf16[224,640]{1,0:T(8,128)(2,1)}, u32[]{:S(2)}) copy-start(bf16[224,640]{1,0:T(8,128)(2,1)} %get-tuple-element.65) | copy-start | bytes 860164
  38.0 19.7 %copy-start.7 = (bf16[224,640]{1,0:T(8,128)(2,1)S(1)}, bf16[224,640]{1,0:T(8,128)(2,1)}, u32[]{:S(2)}) copy-start(bf16[224,640]{1,0:T(8,128)(2,1)} %get-tuple-element.74) | copy-start | bytes 860164
  38.0 89.0 %all-to-all-start.1 = ((bf16[16,24,1024]{2,1,0:T(8,128)(2,1)}), bf16[16,24,1024]{2,1,0:T(8,128)(2,1)S(1)}, u32[]{:S(2)}, u32[]{:S(2)}) async-start(bf16[16,24,1024]{2,1,0:T(8,128)(2,1)} %bitcast.6), calls=%async_computation.1 | async-start | bytes 1572864 | tf_op jit(solution)/shard_map/all_to_all | solution.py:321
  42.9 26.7 %collective-permute-start.4 = (bf16[160,1408]{1,0:T(8,128)(2,1)}, bf16[160,1408]{1,0:T(8,128)(2,1)}, u32[]{:S(2)}, u32[]{:S(2)}) collective-permute-start(bf16[160,1408]{1,0:T(8,128)(2,1)} %collective-permute-done.3), channel_id=1, source_target_pairs={{0,0},{1,4},{2,64},{3,68},{4,128},{5,132},{6,192},{7,196},{8,256},... | collective-permute-start | bytes 1351688 | tf_op jit(solution)/shard_map/ppermute | solution.py:304
  53.5 40.4 %collective-permute-start.1 = (bf16[448,640]{1,0:T(8,128)(2,1)}, bf16[448,640]{1,0:T(8,128)(2,1)S(1)}, u32[]{:S(2)}, u32[]{:S(2)}) collective-permute-start(bf16[448,640]{1,0:T(8,128)(2,1)} %pad_maximum_fusion.4), channel_id=1, source_target_pairs={{0,32},{16,48},{32,0},{48,16},{1,33},{17,49},{33,1},{49,17},{2,34}... | collective-permute-start | bytes 1720328 | tf_op jit(solution)/shard_map/ppermute | solution.py:289
  58.6 44.7 %collective-permute-start.2 = (bf16[448,640]{1,0:T(8,128)(2,1)}, bf16[448,640]{1,0:T(8,128)(2,1)}, u32[]{:S(2)}, u32[]{:S(2)}) collective-permute-start(bf16[448,640]{1,0:T(8,128)(2,1)} %pad_maximum_fusion.5), channel_id=1, source_target_pairs={{0,48},{16,32},{32,16},{48,0},{1,49},{17,33},{33,17},{49,1},{2,50}... | collective-permute-start | bytes 1720328 | tf_op jit(solution)/shard_map/ppermute | solution.py:289
  69.6 53.9 %collective-permute-start.5 = (bf16[160,1408]{1,0:T(8,128)(2,1)}, bf16[160,1408]{1,0:T(8,128)(2,1)}, u32[]{:S(2)}, u32[]{:S(2)}) collective-permute-start(bf16[160,1408]{1,0:T(8,128)(2,1)} %collective-permute-done.4), channel_id=1, source_target_pairs={{0,2},{2,0},{4,6},{6,4},{1,3},{3,1},{5,7},{7,5},{8,10},{10,8},{12,... | collective-permute-start | bytes 1351688 | tf_op jit(solution)/shard_map/ppermute | solution.py:319
  71.6 52.0 %collective-permute-start.6 = (bf16[160,1408]{1,0:T(8,128)(2,1)}, bf16[160,1408]{1,0:T(8,128)(2,1)}, u32[]{:S(2)}, u32[]{:S(2)}) collective-permute-start(bf16[160,1408]{1,0:T(8,128)(2,1)} %collective-permute-done.4), channel_id=1, source_target_pairs={{0,4},{2,6},{4,0},{6,2},{1,5},{3,7},{5,1},{7,3},{8,12},{10,14},{12... | collective-permute-start | bytes 1351688 | tf_op jit(solution)/shard_map/ppermute | solution.py:319
  73.5 50.0 %collective-permute-start.7 = (bf16[160,1408]{1,0:T(8,128)(2,1)}, bf16[160,1408]{1,0:T(8,128)(2,1)}, u32[]{:S(2)}, u32[]{:S(2)}) collective-permute-start(bf16[160,1408]{1,0:T(8,128)(2,1)} %collective-permute-done.4), channel_id=1, source_target_pairs={{0,6},{2,4},{4,2},{6,0},{1,7},{3,5},{5,3},{7,1},{8,14},{10,12},{12... | collective-permute-start | bytes 1351688 | tf_op jit(solution)/shard_map/ppermute | solution.py:319
  104.5 20.7 %copy-start = (bf16[1024,640]{1,0:T(8,128)(2,1)}, bf16[1024,640]{1,0:T(8,128)(2,1)S(1)}, u32[]{:S(2)}) copy-start(bf16[1024,640]{1,0:T(8,128)(2,1)S(1)} %get-tuple-element.36.gate) | copy-start | bytes 3932164
  104.5 20.7 %copy-start.2 = (bf16[1024,640]{1,0:T(8,128)(2,1)}, bf16[1024,640]{1,0:T(8,128)(2,1)S(1)}, u32[]{:S(2)}) copy-start(bf16[1024,640]{1,0:T(8,128)(2,1)S(1)} %get-tuple-element.37.up) | copy-start | bytes 3932164
  127.0 1.3 copy-start.1
  128.3 1.3 copy-start.3
  132.3 45.1 %all-to-all-start.2 = ((bf16[8,64,1280]{2,1,0:T(8,128)(2,1)}), bf16[8,64,1280]{2,1,0:T(8,128)(2,1)S(1)}, u32[]{:S(2)}, u32[]{:S(2)}) async-start(bf16[8,64,1280]{2,1,0:T(8,128)(2,1)} %shard_map.103), calls=%async_computation.2 | async-start | bytes 2621440 | tf_op jit(solution)/shard_map/all_to_all | solution.py:344
  142.5 35.2 %collective-permute-start.10 = (bf16[224,640]{1,0:T(8,128)(2,1)}, bf16[224,640]{1,0:T(8,128)(2,1)}, u32[]{:S(2)}, u32[]{:S(2)}) collective-permute-start(bf16[224,640]{1,0:T(8,128)(2,1)} %get-tuple-element.44), channel_id=1, source_target_pairs={{0,48},{16,32},{32,16},{48,0},{1,49},{17,33},{33,17},{49,1},{2,50}... | collective-permute-start | bytes 860168 | tf_op jit(solution)/shard_map/ppermute | solution.py:289
  144.4 33.3 %collective-permute-start.8 = (bf16[224,640]{1,0:T(8,128)(2,1)}, bf16[224,640]{1,0:T(8,128)(2,1)}, u32[]{:S(2)}, u32[]{:S(2)}) collective-permute-start(bf16[224,640]{1,0:T(8,128)(2,1)} %get-tuple-element.42), channel_id=1, source_target_pairs={{0,16},{16,0},{32,48},{48,32},{1,17},{17,1},{33,49},{49,33},{2,18}... | collective-permute-start | bytes 860168 | tf_op jit(solution)/shard_map/ppermute | solution.py:289
  148.9 28.9 %collective-permute-start.9 = (bf16[224,640]{1,0:T(8,128)(2,1)}, bf16[224,640]{1,0:T(8,128)(2,1)}, u32[]{:S(2)}, u32[]{:S(2)}) collective-permute-start(bf16[224,640]{1,0:T(8,128)(2,1)} %get-tuple-element.43), channel_id=1, source_target_pairs={{0,32},{16,48},{32,0},{48,16},{1,33},{17,49},{33,1},{49,17},{2,34}... | collective-permute-start | bytes 860168 | tf_op jit(solution)/shard_map/ppermute | solution.py:289
  204.6 9.5 %collective-permute-start.11 = (bf16[4,96,224]{2,1,0:T(8,128)(2,1)S(1)}, bf16[4,96,224]{2,1,0:T(8,128)(2,1)S(1)}, u32[]{:S(2)}, u32[]{:S(2)}) collective-permute-start(bf16[4,96,224]{2,1,0:T(8,128)(2,1)S(1)} %get-tuple-element.51), channel_id=1, source_target_pairs={{0,1},{1,0},{2,3},{3,2},{4,5},{5,4},{6,7},{7,6},{8,9},{9,8},{10,11... | collective-permute-start | bytes 516104 | tf_op jit(solution)/shard_map/ppermute | solution.py:247
  206.5 9.6 %collective-permute-start.12 = (bf16[4,96,224]{2,1,0:T(8,128)(2,1)S(1)}, bf16[4,96,224]{2,1,0:T(8,128)(2,1)S(1)}, u32[]{:S(2)}, u32[]{:S(2)}) collective-permute-start(bf16[4,96,224]{2,1,0:T(8,128)(2,1)S(1)} %get-tuple-element.52), channel_id=1, source_target_pairs={{0,8},{8,0},{1,9},{9,1},{2,10},{10,2},{3,11},{11,3},{4,12},{12,4},... | collective-permute-start | bytes 516104 | tf_op jit(solution)/shard_map/ppermute | solution.py:248
  208.4 11.1 %collective-permute-start.13 = (bf16[4,96,224]{2,1,0:T(8,128)(2,1)S(1)}, bf16[4,96,224]{2,1,0:T(8,128)(2,1)S(1)}, u32[]{:S(2)}, u32[]{:S(2)}) collective-permute-start(bf16[4,96,224]{2,1,0:T(8,128)(2,1)S(1)} %get-tuple-element.53), channel_id=1, source_target_pairs={{0,9},{1,8},{8,1},{9,0},{2,11},{3,10},{10,3},{11,2},{4,13},{5,12},... | collective-permute-start | bytes 516104 | tf_op jit(solution)/shard_map/ppermute | solution.py:249

commit v3 on v2

--- a/solution.py
+++ b/solution.py
@@ -207,17 +207,15 @@
         ).astype(BF)
 
 
-def result_kernel(got, slots_out, own_out):
+def result_kernel(got, slots_out):
     total = got[0].astype(F32)
     for k in range(1, YH):
         total = total + got[k].astype(F32)
-    expert = total[: EP * SLOT]
     slot, row = iota((EP * LAND, EP * SLOT), 0), iota((EP * LAND, EP * SLOT), 1)
     group = ((slot.astype(F32) + 0.5) * (1.0 / LAND)).astype(jnp.int32)
     place = slot - LAND * group
     pick = (row == SLOT * group + place) & (place < CAP)
-    slots_out[...] = dot(pick.astype(F32).astype(BF), expert.astype(BF)).astype(BF)
-    own_out[...] = total[EP * SLOT :]
+    slots_out[...] = dot(pick.astype(F32).astype(BF), total.astype(BF)).astype(BF)
 
 
 def turn_pairs():
@@ -363,20 +361,24 @@
         scalars=[me],
         flops=8 * EP * SLOT * HID * FEAT,
     )
-    for sent in from_mates:
-        own_sum = own_sum + sent.astype(F32)
-    partial = jnp.concatenate([partial, own_sum.astype(BF)], axis=1)
     partial = lax.all_to_all(partial, "yh", 0, 0, tiled=True)
-    result, own_sum = call(
+    result = call(
         result_kernel,
-        [struct((EP * LAND, FEAT)), struct((ROWS, FEAT), F32)],
+        [struct((EP * LAND, FEAT))],
         [partial],
         flops=2 * EP * LAND * EP * SLOT * FEAT,
     )
     returned = lax.all_to_all(
         result.reshape(EP, LAND, FEAT), ("yl", "x", "c"), 0, 0, tiled=True
     ).reshape(EP * LAND, FEAT)
-    return (own_sum + dot(mix, returned)).astype(BF)[None]
+
+    for sent in from_mates:
+        own_sum = own_sum + sent.astype(F32)
+    total = lax.dynamic_index_in_dim(own_sum, position, 0, keepdims=False)
+    for k in range(1, YH):
+        piece = lax.dynamic_index_in_dim(own_sum, position ^ k, 0, keepdims=False)
+        total = total + moved(piece.astype(BF), k).astype(F32)
+    return (total + dot(mix, returned)).astype(BF)[None]
 
 
 def solution(mesh):

time: 265 us -> 255 us (0.962)
  blocking collectives: 84.5 us -> 45 us
  starting transfers between devices: 86.9 us -> 111 us
  waiting for transfers between devices: 59.7 us -> 64.6 us
    all_to_all x2 -> x0, blocking collectives: 39.7 us -> none  [the longest x1 26.8 us: local(): partial = lax.all_to_all(partial, 'yh', 0, 0, tiled=True)]
    ppermute x6 -> x9, starting transfers between devices: 23 us -> 36.4 us  [moved(): return lax.ppermute(block, 'yh', [(i, i ^ k) for i in range(YH)])]
    all_to_all x0 -> x2, starting transfers between devices: none -> 10.4 us  [the longest x1 6.93 us: local(): lax.all_to_all(result.reshape(EP, LAND, FEAT), ('yl', 'x', 'c'), 0, 0, ti...]
    all_to_all x0 -> x2, waiting for transfers between devices: none -> 6.95 us  [the longest x1 6.95 us: local(): partial = lax.all_to_all(partial, 'yh', 0, 0, tiled=True)]
    ppermute x1, waiting for transfers between devices: 3.42 us -> 0.01 us  [to_mates(): lax.ppermute(third, ('yl', 'c'), CROSS)]
    ppermute x6 -> x9, waiting for transfers between devices: 20.9 us -> 24.3 us  [moved(): return lax.ppermute(block, 'yh', [(i, i ^ k) for i in range(YH)])]
  transfers between devices with their start and end apart: 17 -> 22, of which waited for: 7 -> 8; matrix products, arithmetic and copies ran while one was open for 4% -> 4% of each run, Pallas kernels for 3% -> 3%
where the time goes in v3:
time: 255 us; the launch traced here: 252 us
  starting transfers between devices  111 us (44%)
  waiting for transfers between devices  64.6 us (25%)
  blocking collectives  45 us (18%)
  Pallas kernels  13.1 us (5%)
  local copies, waits for them, and re-layouts  11 us (4%)
  other arithmetic  6.98 us (3%)
    ppermute x9, starting transfers between devices, moved(): return lax.ppermute(block, 'yh', [(i, i ^ k) for i in range(YH)])  36.4 us
    all_to_all x1, blocking collectives, local(): hidden = lax.all_to_all(hidden, 'z', 0, 0, tiled=True)  25.9 us
    ppermute x9, waiting for transfers between devices, moved(): return lax.ppermute(block, 'yh', [(i, i ^ k) for i in range(YH)])  24.3 us
    all_to_all x1, waiting for transfers between devices, local(): pre = lax.all_to_all(pre, 'z', 0, 0, tiled=True)  22.6 us
    all_gather x1, blocking collectives, local(): mates = [lax.all_gather(own, ('yl', 'c'), axis=0)]  19.2 us
    all_to_all x1, starting transfers between devices, local(): lax.all_to_all(send, ('z', 'yh'), 0, 0, tiled=True).reshape(4 * TP, WIDE)  16.1 us
    pallas_call x8, Pallas kernels, call(): pl.pallas_call(kernel, out_shape=outs[0] if single else outs, in_specs=sp...  13.1 us
    ppermute x3, starting transfers between devices, local(): lax.ppermute(dense, 'x', [(i, i ^ k) for i in range(X)])  10.4 us
  transfers between devices with their start and end apart: 22, of which 8 were waited for; matrix products, arithmetic and copies ran while one was open for 4% of the time, Pallas kernels for 3%

profile of v3, /device:TPU:6, one launch (start us, length us, event | category | flops | bytes accessed | tf_op | source)
XLA Modules:
  0.0 252.0 jit_solution(17990518878592126781)
XLA Ops:
  4.9 16.1 %all-to-all-start = ((bf16[32,4,1024]{2,1,0:T(4,128)(2,1)}), bf16[32,4,1024]{2,1,0:T(4,128)(2,1)}, u32[]{:S(2)}, u32[]{:S(2)}) async-start(bf16[32,4,1024]{2,1,0:T(4,128)(2,1)} %bitcast.6), calls=%async_computation | async-start | bytes 524288 | tf_op jit(solution)/shard_map/all_to_all | solution.py:303
  22.1 5.0 %collective-permute-start.3 = (bf16[160,1408]{1,0:T(8,128)(2,1)}, bf16[160,1408]{1,0:T(8,128)(2,1)}, u32[]{:S(2)}, u32[]{:S(2)}) collective-permute-start(bf16[160,1408]{1,0:T(8,128)(2,1)} %concatenate.24), channel_id=1, source_target_pairs={{0,0},{1,1},{2,2},{3,3},{4,4},{5,5},{6,6},{7,7},{8,8},{9,9},{10,10... | collective-permute-start | bytes 1351688 | tf_op jit(solution)/shard_map/ppermute | solution.py:301
  29.2 4.7 %collective-permute-start = (bf16[448,640]{1,0:T(8,128)(2,1)}, bf16[448,640]{1,0:T(8,128)(2,1)S(1)}, u32[]{:S(2)}, u32[]{:S(2)}) collective-permute-start(bf16[448,640]{1,0:T(8,128)(2,1)} %pad_maximum_fusion.2), channel_id=1, source_target_pairs={{0,16},{16,0},{32,48},{48,32},{1,17},{17,1},{33,49},{49,33},{2,18}... | collective-permute-start | bytes 1720328 | tf_op jit(solution)/shard_map/ppermute | solution.py:287
  38.1 4.8 %all-to-all-start.1 = ((bf16[16,24,1024]{2,1,0:T(8,128)(2,1)}), bf16[16,24,1024]{2,1,0:T(8,128)(2,1)S(1)}, u32[]{:S(2)}, u32[]{:S(2)}) async-start(bf16[16,24,1024]{2,1,0:T(8,128)(2,1)} %bitcast.7), calls=%async_computation.1 | async-start | bytes 1572864 | tf_op jit(solution)/shard_map/all_to_all | solution.py:319
  42.9 9.7 %collective-permute-start.4 = (bf16[160,1408]{1,0:T(8,128)(2,1)}, bf16[160,1408]{1,0:T(8,128)(2,1)}, u32[]{:S(2)}, u32[]{:S(2)}) collective-permute-start(bf16[160,1408]{1,0:T(8,128)(2,1)} %collective-permute-done.3), channel_id=1, source_target_pairs={{0,0},{1,4},{2,64},{3,68},{4,128},{5,132},{6,192},{7,196},{8,256},... | collective-permute-start | bytes 1351688 | tf_op jit(solution)/shard_map/ppermute | solution.py:302
  53.4 4.2 %collective-permute-start.1 = (bf16[448,640]{1,0:T(8,128)(2,1)}, bf16[448,640]{1,0:T(8,128)(2,1)S(1)}, u32[]{:S(2)}, u32[]{:S(2)}) collective-permute-start(bf16[448,640]{1,0:T(8,128)(2,1)} %pad_maximum_fusion.3), channel_id=1, source_target_pairs={{0,32},{16,48},{32,0},{48,16},{1,33},{17,49},{33,1},{49,17},{2,34}... | collective-permute-start | bytes 1720328 | tf_op jit(solution)/shard_map/ppermute | solution.py:287
  58.5 1.9 collective-permute-start.2
  60.4 9.2 %collective-permute-done.4 = bf16[160,1408]{1,0:T(8,128)(2,1)} collective-permute-done((bf16[160,1408]{1,0:T(8,128)(2,1)}, bf16[160,1408]{1,0:T(8,128)(2,1)}, u32[]{:S(2)}, u32[]{:S(2)}) %collective-permute-start.4) | collective-permute-done | bytes 450592 | tf_op jit(solution)/shard_map/ppermute | solution.py:302
  69.6 1.9 collective-permute-start.5
  71.5 1.9 collective-permute-start.6
  73.4 6.6 %collective-permute-start.7 = (bf16[160,1408]{1,0:T(8,128)(2,1)}, bf16[160,1408]{1,0:T(8,128)(2,1)}, u32[]{:S(2)}, u32[]{:S(2)}) collective-permute-start(bf16[160,1408]{1,0:T(8,128)(2,1)} %collective-permute-done.4), channel_id=1, source_target_pairs={{0,6},{2,4},{4,2},{6,0},{1,7},{3,5},{5,3},{7,1},{8,14},{10,12},{12... | collective-permute-start | bytes 1351688 | tf_op jit(solution)/shard_map/ppermute | solution.py:317
  80.1 2.2 dynamic-slice_bitcast_fusion
  82.3 11.4 %collective-permute-done.1.part2 = bf16[448,640]{1,0:T(8,128)(2,1)S(1)} collective-permute-done((bf16[448,640]{1,0:T(8,128)(2,1)}, bf16[448,640]{1,0:T(8,128)(2,1)S(1)}, u32[]{:S(2)}, u32[]{:S(2)}) %collective-permute-start.1) | collective-permute-done | bytes 573472 | tf_op jit(solution)/shard_map/ppermute | solution.py:287
  93.7 9.4 %collective-permute-done.2.part3 = bf16[448,640]{1,0:T(8,128)(2,1)} collective-permute-done((bf16[448,640]{1,0:T(8,128)(2,1)}, bf16[448,640]{1,0:T(8,128)(2,1)}, u32[]{:S(2)}, u32[]{:S(2)}) %collective-permute-start.2) | collective-permute-done | bytes 573472 | tf_op jit(solution)/shard_map/ppermute | solution.py:287
  104.4 19.2 %all-gather = bf16[384,1024]{1,0:T(8,128)(2,1)S(1)} all-gather(bf16[96,1024]{1,0:T(8,128)(2,1)S(1)} %get-tuple-element.33), channel_id=2, replica_groups=mesh['z'=8,'yh'=4,'yl'=2,'x'=4,'c'=2] {'yl','c'}, dimensions={0}, use_global_device_ids=true | all-gather | bytes 983040 | tf_op jit(solution)/shard_map/all_gather | solution.py:312
  129.7 2.6 %shard_map.103 = bf16[8,64,1280]{2,1,0:T(8,128)(2,1)} custom-call(bf16[384,1024]{1,0:T(8,128)(2,1)S(1)} %bitcast.77, bf16[1024,640]{1,0:T(8,128)(2,1)S(1)} %copy-done.1, bf16[1024,640]{1,0:T(8,128)(2,1)S(1)} %copy-done.3, bf16[384,640]{1,0:T(8,128)(2,1)S(1)} %shard_map.102.dense), custom_call_target="tpu_custom_call" | custom-call | flops 838860800 | bytes 5210112 | tf_op jit(solution)/shard_map/pallas_call | solution.py:38
  132.3 10.1 %all-to-all-start.2 = ((bf16[8,64,1280]{2,1,0:T(8,128)(2,1)}), bf16[8,64,1280]{2,1,0:T(8,128)(2,1)S(1)}, u32[]{:S(2)}, u32[]{:S(2)}) async-start(bf16[8,64,1280]{2,1,0:T(8,128)(2,1)} %shard_map.103), calls=%async_computation.2 | async-start | bytes 2621440 | tf_op jit(solution)/shard_map/all_to_all | solution.py:342
  142.5 1.9 collective-permute-start.10
  144.4 4.4 %collective-permute-start.8 = (bf16[224,640]{1,0:T(8,128)(2,1)}, bf16[224,640]{1,0:T(8,128)(2,1)}, u32[]{:S(2)}, u32[]{:S(2)}) collective-permute-start(bf16[224,640]{1,0:T(8,128)(2,1)} %get-tuple-element.40), channel_id=1, source_target_pairs={{0,16},{16,0},{32,48},{48,32},{1,17},{17,1},{33,49},{49,33},{2,18}... | collective-permute-start | bytes 860168 | tf_op jit(solution)/shard_map/ppermute | solution.py:287
  148.8 5.9 %collective-permute-start.9 = (bf16[224,640]{1,0:T(8,128)(2,1)}, bf16[224,640]{1,0:T(8,128)(2,1)}, u32[]{:S(2)}, u32[]{:S(2)}) collective-permute-start(bf16[224,640]{1,0:T(8,128)(2,1)} %get-tuple-element.41), channel_id=1, source_target_pairs={{0,32},{16,48},{32,0},{48,16},{1,33},{17,49},{33,1},{49,17},{2,34}... | collective-permute-start | bytes 860168 | tf_op jit(solution)/shard_map/ppermute | solution.py:287
  154.7 22.6 %all-to-all-done.2.got = bf16[8,64,1280]{2,1,0:T(8,128)(2,1)S(1)} async-done(((bf16[8,64,1280]{2,1,0:T(8,128)(2,1)}), bf16[8,64,1280]{2,1,0:T(8,128)(2,1)S(1)}, u32[]{:S(2)}, u32[]{:S(2)}) %all-to-all-start.2) | async-done | bytes 1310752 | tf_op jit(solution)/shard_map/all_to_all | solution.py:342
  177.7 25.9 %all_to_all.30 = bf16[8,64,640]{2,1,0:T(8,128)(2,1)S(1)} all-to-all(bf16[8,64,640]{2,1,0:T(8,128)(2,1)S(1)} %shard_map.104), channel_id=1, replica_groups=mesh['z'=8,'yh'=4,'yl'=2,'x'=4,'c'=2] {'z'}, dimensions={0} | all-to-all | bytes 1310720 | tf_op jit(solution)/shard_map/all_to_all | solution.py:346
  203.6 2.7 %shard_map.106 = bf16[4,320,224]{2,1,0:T(8,128)(2,1)} custom-call(s32[1]{0:T(128)} %bitcast.1.me, bf16[512,640]{1,0:T(8,128)(2,1)S(1)} %bitcast.79, bf16[224,640]{1,0:T(8,128)(2,1)S(1)} %get-tuple-element.49.part0, bf16[224,640]{1,0:T(8,128)(2,1)} %collective-permute-done.8.part1, bf16[224,640]{1,0:T(8,128)(2,1)} %collective-permute-done.9.part2, ...), custom_call_target="tpu_custom_call" | custom-call | flops 367001600 | bytes 2375680 | tf_op jit(solution)/shard_map/pallas_call | solution.py:38
  206.3 3.5 %all-to-all-start.4 = ((bf16[4,320,224]{2,1,0:T(8,128)(2,1)}), bf16[4,320,224]{2,1,0:T(8,128)(2,1)S(1)}, u32[]{:S(2)}, u32[]{:S(2)}) async-start(bf16[4,320,224]{2,1,0:T(8,128)(2,1)} %shard_map.106), calls=%async_computation.4 | async-start | bytes 1310720 | tf_op jit(solution)/shard_map/all_to_all | solution.py:364
  213.4 1.9 collective-permute-start.12
  215.4 3.7 %collective-permute-start.13 = (bf16[4,96,224]{2,1,0:T(8,128)(2,1)}, bf16[4,96,224]{2,1,0:T(8,128)(2,1)S(1)}, u32[]{:S(2)}, u32[]{:S(2)}) collective-permute-start(bf16[4,96,224]{2,1,0:T(8,128)(2,1)} %get-tuple-element.47), channel_id=1, source_target_pairs={{0,9},{1,8},{8,1},{9,0},{2,11},{3,10},{10,3},{11,2},{4,13},{5,12},... | collective-permute-start | bytes 516104 | tf_op jit(solution)/shard_map/ppermute | solution.py:247
  219.1 6.9 %all-to-all-done.4.got = bf16[4,320,224]{2,1,0:T(8,128)(2,1)S(1)} async-done(((bf16[4,320,224]{2,1,0:T(8,128)(2,1)}), bf16[4,320,224]{2,1,0:T(8,128)(2,1)S(1)}, u32[]{:S(2)}, u32[]{:S(2)}) %all-to-all-start.4) | async-done | bytes 573472 | tf_op jit(solution)/shard_map/all_to_all | solution.py:364
  227.1 6.9 %all-to-all-start.5 = ((bf16[16,24,224]{2,1,0:T(8,128)(2,1)}), bf16[16,24,224]{2,1,0:T(8,128)(2,1)S(1)}, u32[]{:S(2)}, u32[]{:S(2)}) async-start(bf16[16,24,224]{2,1,0:T(8,128)(2,1)} %bitcast.38), calls=%async_computation.5 | async-start | bytes 393216 | tf_op jit(solution)/shard_map/all_to_all | solution.py:371
  234.2 6.0 %collective-permute-start.14 = (bf16[96,224]{1,0:T(8,128)(2,1)S(1)}, bf16[96,224]{1,0:T(8,128)(2,1)S(1)}, u32[]{:S(2)}, u32[]{:S(2)}) collective-permute-start(bf16[96,224]{1,0:T(8,128)(2,1)S(1)} %get-tuple-element.65), channel_id=1, source_target_pairs={{0,16},{16,0},{32,48},{48,32},{1,17},{17,1},{33,49},{49,33},{2,18}... | collective-permute-start | bytes 129032 | tf_op jit(solution)/shard_map/ppermute | solution.py:287
  240.2 3.0 %collective-permute-start.15 = (bf16[96,224]{1,0:T(8,128)(2,1)S(1)}, bf16[96,224]{1,0:T(8,128)(2,1)S(1)}, u32[]{:S(2)}, u32[]{:S(2)}) collective-permute-start(bf16[96,224]{1,0:T(8,128)(2,1)S(1)} %get-tuple-element.67), channel_id=1, source_target_pairs={{0,32},{16,48},{32,0},{48,16},{1,33},{17,49},{33,1},{49,17},{2,34}... | collective-permute-start | bytes 129032 | tf_op jit(solution)/shard_map/ppermute | solution.py:287
  243.2 4.4 %collective-permute-start.16 = (bf16[96,224]{1,0:T(8,128)(2,1)S(1)}, bf16[96,224]{1,0:T(8,128)(2,1)S(1)}, u32[]{:S(2)}, u32[]{:S(2)}) collective-permute-start(bf16[96,224]{1,0:T(8,128)(2,1)S(1)} %get-tuple-element.66), channel_id=1, source_target_pairs={{0,48},{16,32},{32,16},{48,0},{1,49},{17,33},{33,17},{49,1},{2,50}... | collective-permute-start | bytes 129032 | tf_op jit(solution)/shard_map/ppermute | solution.py:287
  247.9 2.3 collective-permute-done.15
  (86 shorter events, 28.3 us)
Async XLA Ops:
  0.0 21.0 %copy-start.14 = (bf16[152,448]{1,0:T(8,128)(2,1)S(1)}, bf16[152,448]{1,0:T(8,128)(2,1)}, u32[]{:S(2)}) copy-start(bf16[152,448]{1,0:T(8,128)(2,1)} %param.16) | copy-start | bytes 408580
  1.0 20.1 %copy-start.15 = (pred[256]{0:T(512)(128)(4,1)S(1)}, pred[256]{0:T(512)(128)(4,1)}, u32[]{:S(2)}) copy-start(pred[256]{0:T(512)(128)(4,1)} %constant.60.clone.1) | copy-start | bytes 772
  2.7 18.4 %copy-start.12 = (bf16[448,152]{0,1:T(8,128)(2,1)S(1)}, bf16[448,152]{0,1:T(8,128)(2,1)}, u32[]{:S(2)}) copy-start(bf16[448,152]{0,1:T(8,128)(2,1)} %param.15) | copy-start | bytes 408580
  2.7 18.4 %copy-start.13 = (bf16[448,152]{0,1:T(8,128)(2,1)S(1)}, bf16[448,152]{0,1:T(8,128)(2,1)}, u32[]{:S(2)}) copy-start(bf16[448,152]{0,1:T(8,128)(2,1)} %param.14) | copy-start | bytes 408580
  4.9 30.5 %all-to-all-start = ((bf16[32,4,1024]{2,1,0:T(4,128)(2,1)}), bf16[32,4,1024]{2,1,0:T(4,128)(2,1)}, u32[]{:S(2)}, u32[]{:S(2)}) async-start(bf16[32,4,1024]{2,1,0:T(4,128)(2,1)} %bitcast.6), calls=%async_computation | async-start | bytes 524288 | tf_op jit(solution)/shard_map/all_to_all | solution.py:303
  22.1 20.7 %collective-permute-start.3 = (bf16[160,1408]{1,0:T(8,128)(2,1)}, bf16[160,1408]{1,0:T(8,128)(2,1)}, u32[]{:S(2)}, u32[]{:S(2)}) collective-permute-start(bf16[160,1408]{1,0:T(8,128)(2,1)} %concatenate.24), channel_id=1, source_target_pairs={{0,0},{1,1},{2,2},{3,3},{4,4},{5,5},{6,6},{7,7},{8,8},{9,9},{10,10... | collective-permute-start | bytes 1351688 | tf_op jit(solution)/shard_map/ppermute | solution.py:301
  29.2 23.4 %copy-start.10 = (bf16[224,640]{1,0:T(8,128)(2,1)S(1)}, bf16[224,640]{1,0:T(8,128)(2,1)}, u32[]{:S(2)}) copy-start(bf16[224,640]{1,0:T(8,128)(2,1)} %get-tuple-element.64) | copy-start | bytes 860164
  29.2 23.4 %copy-start.11 = (bf16[224,640]{1,0:T(8,128)(2,1)S(1)}, bf16[224,640]{1,0:T(8,128)(2,1)}, u32[]{:S(2)}) copy-start(bf16[224,640]{1,0:T(8,128)(2,1)} %get-tuple-element.70) | copy-start | bytes 860164
  29.2 44.3 %collective-permute-start = (bf16[448,640]{1,0:T(8,128)(2,1)}, bf16[448,640]{1,0:T(8,128)(2,1)S(1)}, u32[]{:S(2)}, u32[]{:S(2)}) collective-permute-start(bf16[448,640]{1,0:T(8,128)(2,1)} %pad_maximum_fusion.2), channel_id=1, source_target_pairs={{0,16},{16,0},{32,48},{48,32},{1,17},{17,1},{33,49},{49,33},{2,18}... | collective-permute-start | bytes 1720328 | tf_op jit(solution)/shard_map/ppermute | solution.py:287
  38.0 15.4 %copy-start.4 = (bf16[96,384]{1,0:T(8,128)(2,1)}, bf16[96,384]{1,0:T(8,128)(2,1)S(1)}, u32[]{:S(2)}) copy-start(bf16[96,384]{1,0:T(8,128)(2,1)S(1)} %get-tuple-element.48) | copy-start | bytes 221188
  38.1 89.0 %all-to-all-start.1 = ((bf16[16,24,1024]{2,1,0:T(8,128)(2,1)}), bf16[16,24,1024]{2,1,0:T(8,128)(2,1)S(1)}, u32[]{:S(2)}, u32[]{:S(2)}) async-start(bf16[16,24,1024]{2,1,0:T(8,128)(2,1)} %bitcast.7), calls=%async_computation.1 | async-start | bytes 1572864 | tf_op jit(solution)/shard_map/all_to_all | solution.py:319
  42.9 26.7 %collective-permute-start.4 = (bf16[160,1408]{1,0:T(8,128)(2,1)}, bf16[160,1408]{1,0:T(8,128)(2,1)}, u32[]{:S(2)}, u32[]{:S(2)}) collective-permute-start(bf16[160,1408]{1,0:T(8,128)(2,1)} %collective-permute-done.3), channel_id=1, source_target_pairs={{0,0},{1,4},{2,64},{3,68},{4,128},{5,132},{6,192},{7,196},{8,256},... | collective-permute-start | bytes 1351688 | tf_op jit(solution)/shard_map/ppermute | solution.py:302
  53.4 40.3 %collective-permute-start.1 = (bf16[448,640]{1,0:T(8,128)(2,1)}, bf16[448,640]{1,0:T(8,128)(2,1)S(1)}, u32[]{:S(2)}, u32[]{:S(2)}) collective-permute-start(bf16[448,640]{1,0:T(8,128)(2,1)} %pad_maximum_fusion.3), channel_id=1, source_target_pairs={{0,32},{16,48},{32,0},{48,16},{1,33},{17,49},{33,1},{49,17},{2,34}... | collective-permute-start | bytes 1720328 | tf_op jit(solution)/shard_map/ppermute | solution.py:287
  58.5 44.6 %collective-permute-start.2 = (bf16[448,640]{1,0:T(8,128)(2,1)}, bf16[448,640]{1,0:T(8,128)(2,1)}, u32[]{:S(2)}, u32[]{:S(2)}) collective-permute-start(bf16[448,640]{1,0:T(8,128)(2,1)} %pad_maximum_fusion.4), channel_id=1, source_target_pairs={{0,48},{16,32},{32,16},{48,0},{1,49},{17,33},{33,17},{49,1},{2,50}... | collective-permute-start | bytes 1720328 | tf_op jit(solution)/shard_map/ppermute | solution.py:287
  69.6 54.0 %collective-permute-start.5 = (bf16[160,1408]{1,0:T(8,128)(2,1)}, bf16[160,1408]{1,0:T(8,128)(2,1)}, u32[]{:S(2)}, u32[]{:S(2)}) collective-permute-start(bf16[160,1408]{1,0:T(8,128)(2,1)} %collective-permute-done.4), channel_id=1, source_target_pairs={{0,2},{2,0},{4,6},{6,4},{1,3},{3,1},{5,7},{7,5},{8,10},{10,8},{12,... | collective-permute-start | bytes 1351688 | tf_op jit(solution)/shard_map/ppermute | solution.py:317
  71.5 52.1 %collective-permute-start.6 = (bf16[160,1408]{1,0:T(8,128)(2,1)}, bf16[160,1408]{1,0:T(8,128)(2,1)}, u32[]{:S(2)}, u32[]{:S(2)}) collective-permute-start(bf16[160,1408]{1,0:T(8,128)(2,1)} %collective-permute-done.4), channel_id=1, source_target_pairs={{0,4},{2,6},{4,0},{6,2},{1,5},{3,7},{5,1},{7,3},{8,12},{10,14},{12... | collective-permute-start | bytes 1351688 | tf_op jit(solution)/shard_map/ppermute | solution.py:317
  73.4 50.1 %collective-permute-start.7 = (bf16[160,1408]{1,0:T(8,128)(2,1)}, bf16[160,1408]{1,0:T(8,128)(2,1)}, u32[]{:S(2)}, u32[]{:S(2)}) collective-permute-start(bf16[160,1408]{1,0:T(8,128)(2,1)} %collective-permute-done.4), channel_id=1, source_target_pairs={{0,6},{2,4},{4,2},{6,0},{1,7},{3,5},{5,3},{7,1},{8,14},{10,12},{12... | collective-permute-start | bytes 1351688 | tf_op jit(solution)/shard_map/ppermute | solution.py:317
  104.4 20.9 %copy-start = (bf16[1024,640]{1,0:T(8,128)(2,1)}, bf16[1024,640]{1,0:T(8,128)(2,1)S(1)}, u32[]{:S(2)}) copy-start(bf16[1024,640]{1,0:T(8,128)(2,1)S(1)} %get-tuple-element.34.gate) | copy-start | bytes 3932164
  104.4 20.9 %copy-start.2 = (bf16[1024,640]{1,0:T(8,128)(2,1)}, bf16[1024,640]{1,0:T(8,128)(2,1)S(1)}, u32[]{:S(2)}) copy-start(bf16[1024,640]{1,0:T(8,128)(2,1)S(1)} %get-tuple-element.35.up) | copy-start | bytes 3932164
  132.3 45.0 %all-to-all-start.2 = ((bf16[8,64,1280]{2,1,0:T(8,128)(2,1)}), bf16[8,64,1280]{2,1,0:T(8,128)(2,1)S(1)}, u32[]{:S(2)}, u32[]{:S(2)}) async-start(bf16[8,64,1280]{2,1,0:T(8,128)(2,1)} %shard_map.103), calls=%async_computation.2 | async-start | bytes 2621440 | tf_op jit(solution)/shard_map/all_to_all | solution.py:342
  142.5 35.2 %collective-permute-start.10 = (bf16[224,640]{1,0:T(8,128)(2,1)}, bf16[224,640]{1,0:T(8,128)(2,1)}, u32[]{:S(2)}, u32[]{:S(2)}) collective-permute-start(bf16[224,640]{1,0:T(8,128)(2,1)} %get-tuple-element.42), channel_id=1, source_target_pairs={{0,48},{16,32},{32,16},{48,0},{1,49},{17,33},{33,17},{49,1},{2,50}... | collective-permute-start | bytes 860168 | tf_op jit(solution)/shard_map/ppermute | solution.py:287
  144.4 33.3 %collective-permute-start.8 = (bf16[224,640]{1,0:T(8,128)(2,1)}, bf16[224,640]{1,0:T(8,128)(2,1)}, u32[]{:S(2)}, u32[]{:S(2)}) collective-permute-start(bf16[224,640]{1,0:T(8,128)(2,1)} %get-tuple-element.40), channel_id=1, source_target_pairs={{0,16},{16,0},{32,48},{48,32},{1,17},{17,1},{33,49},{49,33},{2,18}... | collective-permute-start | bytes 860168 | tf_op jit(solution)/shard_map/ppermute | solution.py:287
  148.8 28.9 %collective-permute-start.9 = (bf16[224,640]{1,0:T(8,128)(2,1)}, bf16[224,640]{1,0:T(8,128)(2,1)}, u32[]{:S(2)}, u32[]{:S(2)}) collective-permute-start(bf16[224,640]{1,0:T(8,128)(2,1)} %get-tuple-element.41), channel_id=1, source_target_pairs={{0,32},{16,48},{32,0},{48,16},{1,33},{17,49},{33,1},{49,17},{2,34}... | collective-permute-start | bytes 860168 | tf_op jit(solution)/shard_map/ppermute | solution.py:287
  206.3 19.8 %all-to-all-start.4 = ((bf16[4,320,224]{2,1,0:T(8,128)(2,1)}), bf16[4,320,224]{2,1,0:T(8,128)(2,1)S(1)}, u32[]{:S(2)}, u32[]{:S(2)}) async-start(bf16[4,320,224]{2,1,0:T(8,128)(2,1)} %shard_map.106), calls=%async_computation.4 | async-start | bytes 1310720 | tf_op jit(solution)/shard_map/all_to_all | solution.py:364
  211.5 22.5 %collective-permute-start.11 = (bf16[4,96,224]{2,1,0:T(8,128)(2,1)}, bf16[4,96,224]{2,1,0:T(8,128)(2,1)S(1)}, u32[]{:S(2)}, u32[]{:S(2)}) collective-permute-start(bf16[4,96,224]{2,1,0:T(8,128)(2,1)} %get-tuple-element.45), channel_id=1, source_target_pairs={{0,1},{1,0},{2,3},{3,2},{4,5},{5,4},{6,7},{7,6},{8,9},{9,8},{10,11... | collective-permute-start | bytes 516104 | tf_op jit(solution)/shard_map/ppermute | solution.py:245
  213.4 20.6 %collective-permute-start.12 = (bf16[4,96,224]{2,1,0:T(8,128)(2,1)}, bf16[4,96,224]{2,1,0:T(8,128)(2,1)S(1)}, u32[]{:S(2)}, u32[]{:S(2)}) collective-permute-start(bf16[4,96,224]{2,1,0:T(8,128)(2,1)} %get-tuple-element.46), channel_id=1, source_target_pairs={{0,8},{8,0},{1,9},{9,1},{2,10},{10,2},{3,11},{11,3},{4,12},{12,4},... | collective-permute-start | bytes 516104 | tf_op jit(solution)/shard_map/ppermute | solution.py:246
  215.4 18.7 %collective-permute-start.13 = (bf16[4,96,224]{2,1,0:T(8,128)(2,1)}, bf16[4,96,224]{2,1,0:T(8,128)(2,1)S(1)}, u32[]{:S(2)}, u32[]{:S(2)}) collective-permute-start(bf16[4,96,224]{2,1,0:T(8,128)(2,1)} %get-tuple-element.47), channel_id=1, source_target_pairs={{0,9},{1,8},{8,1},{9,0},{2,11},{3,10},{10,3},{11,2},{4,13},{5,12},... | collective-permute-start | bytes 516104 | tf_op jit(solution)/shard_map/ppermute | solution.py:247
  227.1 20.6 %copy-start.5 = (bf16[96,384]{1,0:T(8,128)(2,1)S(1)}, bf16[96,384]{1,0:T(8,128)(2,1)}, u32[]{:S(2)}) copy-start(bf16[96,384]{1,0:T(8,128)(2,1)} %copy-done.4) | copy-start | bytes 221188
  227.1 20.6 %all-to-all-start.5 = ((bf16[16,24,224]{2,1,0:T(8,128)(2,1)}), bf16[16,24,224]{2,1,0:T(8,128)(2,1)S(1)}, u32[]{:S(2)}, u32[]{:S(2)}) async-start(bf16[16,24,224]{2,1,0:T(8,128)(2,1)} %bitcast.38), calls=%async_computation.5 | async-start | bytes 393216 | tf_op jit(solution)/shard_map/all_to_all | solution.py:371
  234.2 13.7 %collective-permute-start.14 = (bf16[96,224]{1,0:T(8,128)(2,1)S(1)}, bf16[96,224]{1,0:T(8,128)(2,1)S(1)}, u32[]{:S(2)}, u32[]{:S(2)}) collective-permute-start(bf16[96,224]{1,0:T(8,128)(2,1)S(1)} %get-tuple-element.65), channel_id=1, source_target_pairs={{0,16},{16,0},{32,48},{48,32},{1,17},{17,1},{33,49},{49,33},{2,18}... | collective-permute-start | bytes 129032 | tf_op jit(solution)/shard_map/ppermute | solution.py:287
  240.2 10.0 %collective-permute-start.15 = (bf16[96,224]{1,0:T(8,128)(2,1)S(1)}, bf16[96,224]{1,0:T(8,128)(2,1)S(1)}, u32[]{:S(2)}, u32[]{:S(2)}) collective-permute-start(bf16[96,224]{1,0:T(8,128)(2,1)S(1)} %get-tuple-element.67), channel_id=1, source_target_pairs={{0,32},{16,48},{32,0},{48,16},{1,33},{17,49},{33,1},{49,17},{2,34}... | collective-permute-start | bytes 129032 | tf_op jit(solution)/shard_map/ppermute | solution.py:287
  243.2 8.1 %collective-permute-start.16 = (bf16[96,224]{1,0:T(8,128)(2,1)S(1)}, bf16[96,224]{1,0:T(8,128)(2,1)S(1)}, u32[]{:S(2)}, u32[]{:S(2)}) collective-permute-start(bf16[96,224]{1,0:T(8,128)(2,1)S(1)} %get-tuple-element.66), channel_id=1, source_target_pairs={{0,48},{16,32},{32,16},{48,0},{1,49},{17,33},{33,17},{49,1},{2,50}... | collective-permute-start | bytes 129032 | tf_op jit(solution)/shard_map/ppermute | solution.py:287
  (6 other events, 44.3 us)

commit v4 on v3

--- a/solution.py
+++ b/solution.py
@@ -342,7 +342,7 @@
     pre = lax.all_to_all(pre, "z", 0, 0, tiled=True)
     hidden = call(hidden_kernel, [struct((Z, ROW_Z, HID))], [pre], scalars=[me])
     downs[1:] = [moved(downs[k], k) for k in range(1, YH)]
-    hidden, *downs = lax.optimization_barrier((hidden, *downs))
+    hidden, downs[2] = lax.optimization_barrier((hidden, downs[2]))
     hidden = lax.all_to_all(hidden, "z", 0, 0, tiled=True)
     hidden = hidden.reshape(Z * ROW_Z, HID)
     own_sum, *others = call(

time: 255 us -> 256 us (level)
  blocking collectives: 45 us -> 19.1 us
  waiting for transfers between devices: 64.6 us -> 90.4 us
    all_to_all x1 -> x0, blocking collectives: 25.9 us -> none  [local(): hidden = lax.all_to_all(hidden, 'z', 0, 0, tiled=True)]
    ppermute x9, waiting for transfers between devices: 24.3 us -> 37.1 us  [moved(): return lax.ppermute(block, 'yh', [(i, i ^ k) for i in range(YH)])]
    all_to_all x1, waiting for transfers between devices: 22.6 us -> 31 us  [local(): pre = lax.all_to_all(pre, 'z', 0, 0, tiled=True)]
    all_to_all x1, waiting for transfers between devices: 6.95 us -> 11.6 us  [local(): partial = lax.all_to_all(partial, 'yh', 0, 0, tiled=True)]
    all_to_all x0 -> x1, starting transfers between devices: none -> 3.54 us  [local(): hidden = lax.all_to_all(hidden, 'z', 0, 0, tiled=True)]
    ppermute x9, starting transfers between devices: 36.4 us -> 33.2 us  [moved(): return lax.ppermute(block, 'yh', [(i, i ^ k) for i in range(YH)])]
  transfers between devices with their start and end apart: 22 -> 23, of which waited for: 8 -> 9; matrix products, arithmetic and copies ran while one was open for 4% -> 4% of each run, Pallas kernels for 3% -> 3%
where the time goes in v4:
time: 256 us; the launch traced here: 254 us
  starting transfers between devices  112 us (44%)
  waiting for transfers between devices  90.4 us (35%)
  blocking collectives  19.1 us (7%)
  Pallas kernels  12.9 us (5%)
  local copies, waits for them, and re-layouts  11.9 us (5%)
  other arithmetic  7 us (3%)
    ppermute x9, waiting for transfers between devices, moved(): return lax.ppermute(block, 'yh', [(i, i ^ k) for i in range(YH)])  37.1 us
    ppermute x9, starting transfers between devices, moved(): return lax.ppermute(block, 'yh', [(i, i ^ k) for i in range(YH)])  33.2 us
    all_to_all x1, waiting for transfers between devices, local(): pre = lax.all_to_all(pre, 'z', 0, 0, tiled=True)  31 us
    all_gather x1, blocking collectives, local(): mates = [lax.all_gather(own, ('yl', 'c'), axis=0)]  19.1 us
    all_to_all x1, starting transfers between devices, local(): lax.all_to_all(send, ('z', 'yh'), 0, 0, tiled=True).reshape(4 * TP, WIDE)  16.1 us
    pallas_call x8, Pallas kernels, call(): pl.pallas_call(kernel, out_shape=outs[0] if single else outs, in_specs=sp...  12.9 us
    all_to_all x1, waiting for transfers between devices, local(): partial = lax.all_to_all(partial, 'yh', 0, 0, tiled=True)  11.6 us
    ppermute x3, starting transfers between devices, local(): lax.ppermute(dense, 'x', [(i, i ^ k) for i in range(X)])  10.4 us
  transfers between devices with their start and end apart: 23, of which 9 were waited for; matrix products, arithmetic and copies ran while one was open for 4% of the time, Pallas kernels for 3%

profile of v4, /device:TPU:6, one launch (start us, length us, event | category | flops | bytes accessed | tf_op | source)
XLA Modules:
  0.0 253.7 jit_solution(14268997851513063004)
XLA Ops:
  4.9 16.1 %all-to-all-start = ((bf16[32,4,1024]{2,1,0:T(4,128)(2,1)}), bf16[32,4,1024]{2,1,0:T(4,128)(2,1)}, u32[]{:S(2)}, u32[]{:S(2)}) async-start(bf16[32,4,1024]{2,1,0:T(4,128)(2,1)} %bitcast.6), calls=%async_computation | async-start | bytes 524288 | tf_op jit(solution)/shard_map/all_to_all | solution.py:303
  22.1 5.1 %collective-permute-start.3 = (bf16[160,1408]{1,0:T(8,128)(2,1)}, bf16[160,1408]{1,0:T(8,128)(2,1)}, u32[]{:S(2)}, u32[]{:S(2)}) collective-permute-start(bf16[160,1408]{1,0:T(8,128)(2,1)} %concatenate.24), channel_id=1, source_target_pairs={{0,0},{1,1},{2,2},{3,3},{4,4},{5,5},{6,6},{7,7},{8,8},{9,9},{10,10... | collective-permute-start | bytes 1351688 | tf_op jit(solution)/shard_map/ppermute | solution.py:301
  29.3 4.7 %collective-permute-start = (bf16[448,640]{1,0:T(8,128)(2,1)}, bf16[448,640]{1,0:T(8,128)(2,1)S(1)}, u32[]{:S(2)}, u32[]{:S(2)}) collective-permute-start(bf16[448,640]{1,0:T(8,128)(2,1)} %pad_maximum_fusion.2), channel_id=1, source_target_pairs={{0,16},{16,0},{32,48},{48,32},{1,17},{17,1},{33,49},{49,33},{2,18}... | collective-permute-start | bytes 1720328 | tf_op jit(solution)/shard_map/ppermute | solution.py:287
  38.1 4.8 %all-to-all-start.1 = ((bf16[16,24,1024]{2,1,0:T(8,128)(2,1)}), bf16[16,24,1024]{2,1,0:T(8,128)(2,1)S(1)}, u32[]{:S(2)}, u32[]{:S(2)}) async-start(bf16[16,24,1024]{2,1,0:T(8,128)(2,1)} %bitcast.7), calls=%async_computation.1 | async-start | bytes 1572864 | tf_op jit(solution)/shard_map/all_to_all | solution.py:319
  42.9 9.6 %collective-permute-start.4 = (bf16[160,1408]{1,0:T(8,128)(2,1)}, bf16[160,1408]{1,0:T(8,128)(2,1)}, u32[]{:S(2)}, u32[]{:S(2)}) collective-permute-start(bf16[160,1408]{1,0:T(8,128)(2,1)} %collective-permute-done.3), channel_id=1, source_target_pairs={{0,0},{1,4},{2,64},{3,68},{4,128},{5,132},{6,192},{7,196},{8,256},... | collective-permute-start | bytes 1351688 | tf_op jit(solution)/shard_map/ppermute | solution.py:302
  53.4 4.2 %collective-permute-start.1 = (bf16[448,640]{1,0:T(8,128)(2,1)}, bf16[448,640]{1,0:T(8,128)(2,1)S(1)}, u32[]{:S(2)}, u32[]{:S(2)}) collective-permute-start(bf16[448,640]{1,0:T(8,128)(2,1)} %pad_maximum_fusion.3), channel_id=1, source_target_pairs={{0,32},{16,48},{32,0},{48,16},{1,33},{17,49},{33,1},{49,17},{2,34}... | collective-permute-start | bytes 1720328 | tf_op jit(solution)/shard_map/ppermute | solution.py:287
  60.4 9.2 %collective-permute-done.4 = bf16[160,1408]{1,0:T(8,128)(2,1)} collective-permute-done((bf16[160,1408]{1,0:T(8,128)(2,1)}, bf16[160,1408]{1,0:T(8,128)(2,1)}, u32[]{:S(2)}, u32[]{:S(2)}) %collective-permute-start.4) | collective-permute-done | bytes 450592 | tf_op jit(solution)/shard_map/ppermute | solution.py:302
  71.5 1.9 collective-permute-start.6
  73.5 6.6 %collective-permute-start.7 = (bf16[160,1408]{1,0:T(8,128)(2,1)}, bf16[160,1408]{1,0:T(8,128)(2,1)}, u32[]{:S(2)}, u32[]{:S(2)}) collective-permute-start(bf16[160,1408]{1,0:T(8,128)(2,1)} %collective-permute-done.4), channel_id=1, source_target_pairs={{0,6},{2,4},{4,2},{6,0},{1,7},{3,5},{5,3},{7,1},{8,14},{10,12},{12... | collective-permute-start | bytes 1351688 | tf_op jit(solution)/shard_map/ppermute | solution.py:317
  80.1 2.2 dynamic-slice_bitcast_fusion
  82.3 11.4 %collective-permute-done.1.part2 = bf16[448,640]{1,0:T(8,128)(2,1)S(1)} collective-permute-done((bf16[448,640]{1,0:T(8,128)(2,1)}, bf16[448,640]{1,0:T(8,128)(2,1)S(1)}, u32[]{:S(2)}, u32[]{:S(2)}) %collective-permute-start.1) | collective-permute-done | bytes 573472 | tf_op jit(solution)/shard_map/ppermute | solution.py:287
  93.7 9.5 %collective-permute-done.2.part3 = bf16[448,640]{1,0:T(8,128)(2,1)} collective-permute-done((bf16[448,640]{1,0:T(8,128)(2,1)}, bf16[448,640]{1,0:T(8,128)(2,1)}, u32[]{:S(2)}, u32[]{:S(2)}) %collective-permute-start.2) | collective-permute-done | bytes 573472 | tf_op jit(solution)/shard_map/ppermute | solution.py:287
  104.5 19.1 %all-gather = bf16[384,1024]{1,0:T(8,128)(2,1)S(1)} all-gather(bf16[96,1024]{1,0:T(8,128)(2,1)S(1)} %get-tuple-element.30), channel_id=2, replica_groups=mesh['z'=8,'yh'=4,'yl'=2,'x'=4,'c'=2] {'yl','c'}, dimensions={0}, use_global_device_ids=true | all-gather | bytes 983040 | tf_op jit(solution)/shard_map/all_gather | solution.py:312
  129.7 2.6 %shard_map.103 = bf16[8,64,1280]{2,1,0:T(8,128)(2,1)} custom-call(bf16[384,1024]{1,0:T(8,128)(2,1)S(1)} %bitcast.77, bf16[1024,640]{1,0:T(8,128)(2,1)S(1)} %copy-done.2, bf16[1024,640]{1,0:T(8,128)(2,1)S(1)} %copy-done.4, bf16[384,640]{1,0:T(8,128)(2,1)S(1)} %shard_map.102.dense), custom_call_target="tpu_custom_call" | custom-call | flops 838860800 | bytes 5210112 | tf_op jit(solution)/shard_map/pallas_call | solution.py:38
  132.3 10.2 %all-to-all-start.2 = ((bf16[8,64,1280]{2,1,0:T(8,128)(2,1)}), bf16[8,64,1280]{2,1,0:T(8,128)(2,1)S(1)}, u32[]{:S(2)}, u32[]{:S(2)}) async-start(bf16[8,64,1280]{2,1,0:T(8,128)(2,1)} %shard_map.103), calls=%async_computation.2 | async-start | bytes 2621440 | tf_op jit(solution)/shard_map/all_to_all | solution.py:342
  142.5 3.9 %collective-permute-start.8 = (bf16[224,640]{1,0:T(8,128)(2,1)}, bf16[224,640]{1,0:T(8,128)(2,1)}, u32[]{:S(2)}, u32[]{:S(2)}) collective-permute-start(bf16[224,640]{1,0:T(8,128)(2,1)} %get-tuple-element.36), channel_id=1, source_target_pairs={{0,32},{16,48},{32,0},{48,16},{1,33},{17,49},{33,1},{49,17},{2,34}... | collective-permute-start | bytes 860168 | tf_op jit(solution)/shard_map/ppermute | solution.py:287
  146.4 31.0 %all-to-all-done.2.got = bf16[8,64,1280]{2,1,0:T(8,128)(2,1)S(1)} async-done(((bf16[8,64,1280]{2,1,0:T(8,128)(2,1)}), bf16[8,64,1280]{2,1,0:T(8,128)(2,1)S(1)}, u32[]{:S(2)}, u32[]{:S(2)}) %all-to-all-start.2) | async-done | bytes 1310752 | tf_op jit(solution)/shard_map/all_to_all | solution.py:342
  178.6 3.5 %all-to-all-start.3 = ((bf16[8,64,640]{2,1,0:T(8,128)(2,1)}), bf16[8,64,640]{2,1,0:T(8,128)(2,1)S(1)}, u32[]{:S(2)}, u32[]{:S(2)}) async-start(bf16[8,64,640]{2,1,0:T(8,128)(2,1)} %copy-done), calls=%async_computation.3 | async-start | bytes 1310720 | tf_op jit(solution)/shard_map/all_to_all | solution.py:346
  182.1 1.9 collective-permute-start.15
  184.1 4.4 %collective-permute-start.16 = (bf16[224,640]{1,0:T(8,128)(2,1)}, bf16[224,640]{1,0:T(8,128)(2,1)S(1)}, u32[]{:S(2)}, u32[]{:S(2)}) collective-permute-start(bf16[224,640]{1,0:T(8,128)(2,1)} %get-tuple-element.46), channel_id=1, source_target_pairs={{0,48},{16,32},{32,16},{48,0},{1,49},{17,33},{33,17},{49,1},{2,50}... | collective-permute-start | bytes 860168 | tf_op jit(solution)/shard_map/ppermute | solution.py:287
  188.5 11.6 %collective-permute-done.15.part1 = bf16[224,640]{1,0:T(8,128)(2,1)S(1)} collective-permute-done((bf16[224,640]{1,0:T(8,128)(2,1)}, bf16[224,640]{1,0:T(8,128)(2,1)S(1)}, u32[]{:S(2)}, u32[]{:S(2)}) %collective-permute-start.15) | collective-permute-done | bytes 286752 | tf_op jit(solution)/shard_map/ppermute | solution.py:287
  200.0 2.8 %collective-permute-done.16.part3 = bf16[224,640]{1,0:T(8,128)(2,1)S(1)} collective-permute-done((bf16[224,640]{1,0:T(8,128)(2,1)}, bf16[224,640]{1,0:T(8,128)(2,1)S(1)}, u32[]{:S(2)}, u32[]{:S(2)}) %collective-permute-start.16) | collective-permute-done | bytes 286752 | tf_op jit(solution)/shard_map/ppermute | solution.py:287
  202.8 2.5 shard_map.106
  205.4 3.6 %all-to-all-start.4 = ((bf16[4,320,224]{2,1,0:T(8,128)(2,1)}), bf16[4,320,224]{2,1,0:T(8,128)(2,1)S(1)}, u32[]{:S(2)}, u32[]{:S(2)}) async-start(bf16[4,320,224]{2,1,0:T(8,128)(2,1)} %shard_map.106), calls=%async_computation.4 | async-start | bytes 1310720 | tf_op jit(solution)/shard_map/all_to_all | solution.py:364
  210.8 3.1 %collective-permute-start.10 = (bf16[4,96,224]{2,1,0:T(8,128)(2,1)}, bf16[4,96,224]{2,1,0:T(8,128)(2,1)S(1)}, u32[]{:S(2)}, u32[]{:S(2)}) collective-permute-start(bf16[4,96,224]{2,1,0:T(8,128)(2,1)} %get-tuple-element.40), channel_id=1, source_target_pairs={{0,8},{8,0},{1,9},{9,1},{2,10},{10,2},{3,11},{11,3},{4,12},{12,4},... | collective-permute-start | bytes 516104 | tf_op jit(solution)/shard_map/ppermute | solution.py:246
  213.9 1.9 collective-permute-start.11
  215.8 2.8 %collective-permute-start.9 = (bf16[4,96,224]{2,1,0:T(8,128)(2,1)}, bf16[4,96,224]{2,1,0:T(8,128)(2,1)S(1)}, u32[]{:S(2)}, u32[]{:S(2)}) collective-permute-start(bf16[4,96,224]{2,1,0:T(8,128)(2,1)} %get-tuple-element.39), channel_id=1, source_target_pairs={{0,1},{1,0},{2,3},{3,2},{4,5},{5,4},{6,7},{7,6},{8,9},{9,8},{10,11... | collective-permute-start | bytes 516104 | tf_op jit(solution)/shard_map/ppermute | solution.py:245
  218.7 11.6 %all-to-all-done.4.got = bf16[4,320,224]{2,1,0:T(8,128)(2,1)S(1)} async-done(((bf16[4,320,224]{2,1,0:T(8,128)(2,1)}), bf16[4,320,224]{2,1,0:T(8,128)(2,1)S(1)}, u32[]{:S(2)}, u32[]{:S(2)}) %all-to-all-start.4) | async-done | bytes 573472 | tf_op jit(solution)/shard_map/all_to_all | solution.py:364
  231.3 7.3 %all-to-all-start.5 = ((bf16[16,24,224]{2,1,0:T(8,128)(2,1)}), bf16[16,24,224]{2,1,0:T(8,128)(2,1)S(1)}, u32[]{:S(2)}, u32[]{:S(2)}) async-start(bf16[16,24,224]{2,1,0:T(8,128)(2,1)} %bitcast.38), calls=%async_computation.5 | async-start | bytes 393216 | tf_op jit(solution)/shard_map/all_to_all | solution.py:371
  238.7 2.5 collective-permute-start.12
  241.2 3.5 %collective-permute-start.13 = (bf16[96,224]{1,0:T(8,128)(2,1)S(1)}, bf16[96,224]{1,0:T(8,128)(2,1)S(1)}, u32[]{:S(2)}, u32[]{:S(2)}) collective-permute-start(bf16[96,224]{1,0:T(8,128)(2,1)S(1)} %get-tuple-element.61), channel_id=1, source_target_pairs={{0,32},{16,48},{32,0},{48,16},{1,33},{17,49},{33,1},{49,17},{2,34}... | collective-permute-start | bytes 129032 | tf_op jit(solution)/shard_map/ppermute | solution.py:287
  244.8 6.2 %collective-permute-start.14 = (bf16[96,224]{1,0:T(8,128)(2,1)S(1)}, bf16[96,224]{1,0:T(8,128)(2,1)S(1)}, u32[]{:S(2)}, u32[]{:S(2)}) collective-permute-start(bf16[96,224]{1,0:T(8,128)(2,1)S(1)} %get-tuple-element.60), channel_id=1, source_target_pairs={{0,48},{16,32},{32,16},{48,0},{1,49},{17,33},{33,17},{49,1},{2,50}... | collective-permute-start | bytes 129032 | tf_op jit(solution)/shard_map/ppermute | solution.py:287
  (89 shorter events, 31.8 us)
Async XLA Ops:
  0.0 21.0 %copy-start.15 = (bf16[152,448]{1,0:T(8,128)(2,1)S(1)}, bf16[152,448]{1,0:T(8,128)(2,1)}, u32[]{:S(2)}) copy-start(bf16[152,448]{1,0:T(8,128)(2,1)} %param.16) | copy-start | bytes 408580
  1.0 20.2 %copy-start.16 = (pred[256]{0:T(512)(128)(4,1)S(1)}, pred[256]{0:T(512)(128)(4,1)}, u32[]{:S(2)}) copy-start(pred[256]{0:T(512)(128)(4,1)} %constant.60.clone.1) | copy-start | bytes 772
  2.7 18.5 %copy-start.13 = (bf16[448,152]{0,1:T(8,128)(2,1)S(1)}, bf16[448,152]{0,1:T(8,128)(2,1)}, u32[]{:S(2)}) copy-start(bf16[448,152]{0,1:T(8,128)(2,1)} %param.15) | copy-start | bytes 408580
  2.7 18.5 %copy-start.14 = (bf16[448,152]{0,1:T(8,128)(2,1)S(1)}, bf16[448,152]{0,1:T(8,128)(2,1)}, u32[]{:S(2)}) copy-start(bf16[448,152]{0,1:T(8,128)(2,1)} %param.14) | copy-start | bytes 408580
  4.9 30.5 %all-to-all-start = ((bf16[32,4,1024]{2,1,0:T(4,128)(2,1)}), bf16[32,4,1024]{2,1,0:T(4,128)(2,1)}, u32[]{:S(2)}, u32[]{:S(2)}) async-start(bf16[32,4,1024]{2,1,0:T(4,128)(2,1)} %bitcast.6), calls=%async_computation | async-start | bytes 524288 | tf_op jit(solution)/shard_map/all_to_all | solution.py:303
  22.1 20.7 %collective-permute-start.3 = (bf16[160,1408]{1,0:T(8,128)(2,1)}, bf16[160,1408]{1,0:T(8,128)(2,1)}, u32[]{:S(2)}, u32[]{:S(2)}) collective-permute-start(bf16[160,1408]{1,0:T(8,128)(2,1)} %concatenate.24), channel_id=1, source_target_pairs={{0,0},{1,1},{2,2},{3,3},{4,4},{5,5},{6,6},{7,7},{8,8},{9,9},{10,10... | collective-permute-start | bytes 1351688 | tf_op jit(solution)/shard_map/ppermute | solution.py:301
  29.2 23.3 %copy-start.11 = (bf16[224,640]{1,0:T(8,128)(2,1)S(1)}, bf16[224,640]{1,0:T(8,128)(2,1)}, u32[]{:S(2)}) copy-start(bf16[224,640]{1,0:T(8,128)(2,1)} %get-tuple-element.58) | copy-start | bytes 860164
  29.2 23.3 %copy-start.12 = (bf16[224,640]{1,0:T(8,128)(2,1)S(1)}, bf16[224,640]{1,0:T(8,128)(2,1)}, u32[]{:S(2)}) copy-start(bf16[224,640]{1,0:T(8,128)(2,1)} %get-tuple-element.64) | copy-start | bytes 860164
  29.3 44.2 %collective-permute-start = (bf16[448,640]{1,0:T(8,128)(2,1)}, bf16[448,640]{1,0:T(8,128)(2,1)S(1)}, u32[]{:S(2)}, u32[]{:S(2)}) collective-permute-start(bf16[448,640]{1,0:T(8,128)(2,1)} %pad_maximum_fusion.2), channel_id=1, source_target_pairs={{0,16},{16,0},{32,48},{48,32},{1,17},{17,1},{33,49},{49,33},{2,18}... | collective-permute-start | bytes 1720328 | tf_op jit(solution)/shard_map/ppermute | solution.py:287
  38.1 89.0 %all-to-all-start.1 = ((bf16[16,24,1024]{2,1,0:T(8,128)(2,1)}), bf16[16,24,1024]{2,1,0:T(8,128)(2,1)S(1)}, u32[]{:S(2)}, u32[]{:S(2)}) async-start(bf16[16,24,1024]{2,1,0:T(8,128)(2,1)} %bitcast.7), calls=%async_computation.1 | async-start | bytes 1572864 | tf_op jit(solution)/shard_map/all_to_all | solution.py:319
  42.9 26.7 %collective-permute-start.4 = (bf16[160,1408]{1,0:T(8,128)(2,1)}, bf16[160,1408]{1,0:T(8,128)(2,1)}, u32[]{:S(2)}, u32[]{:S(2)}) collective-permute-start(bf16[160,1408]{1,0:T(8,128)(2,1)} %collective-permute-done.3), channel_id=1, source_target_pairs={{0,0},{1,4},{2,64},{3,68},{4,128},{5,132},{6,192},{7,196},{8,256},... | collective-permute-start | bytes 1351688 | tf_op jit(solution)/shard_map/ppermute | solution.py:302
  53.4 40.3 %collective-permute-start.1 = (bf16[448,640]{1,0:T(8,128)(2,1)}, bf16[448,640]{1,0:T(8,128)(2,1)S(1)}, u32[]{:S(2)}, u32[]{:S(2)}) collective-permute-start(bf16[448,640]{1,0:T(8,128)(2,1)} %pad_maximum_fusion.3), channel_id=1, source_target_pairs={{0,32},{16,48},{32,0},{48,16},{1,33},{17,49},{33,1},{49,17},{2,34}... | collective-permute-start | bytes 1720328 | tf_op jit(solution)/shard_map/ppermute | solution.py:287
  58.5 44.7 %collective-permute-start.2 = (bf16[448,640]{1,0:T(8,128)(2,1)}, bf16[448,640]{1,0:T(8,128)(2,1)}, u32[]{:S(2)}, u32[]{:S(2)}) collective-permute-start(bf16[448,640]{1,0:T(8,128)(2,1)} %pad_maximum_fusion.4), channel_id=1, source_target_pairs={{0,48},{16,32},{32,16},{48,0},{1,49},{17,33},{33,17},{49,1},{2,50}... | collective-permute-start | bytes 1720328 | tf_op jit(solution)/shard_map/ppermute | solution.py:287
  69.6 54.0 %collective-permute-start.5 = (bf16[160,1408]{1,0:T(8,128)(2,1)}, bf16[160,1408]{1,0:T(8,128)(2,1)}, u32[]{:S(2)}, u32[]{:S(2)}) collective-permute-start(bf16[160,1408]{1,0:T(8,128)(2,1)} %collective-permute-done.4), channel_id=1, source_target_pairs={{0,2},{2,0},{4,6},{6,4},{1,3},{3,1},{5,7},{7,5},{8,10},{10,8},{12,... | collective-permute-start | bytes 1351688 | tf_op jit(solution)/shard_map/ppermute | solution.py:317
  71.5 52.1 %collective-permute-start.6 = (bf16[160,1408]{1,0:T(8,128)(2,1)}, bf16[160,1408]{1,0:T(8,128)(2,1)}, u32[]{:S(2)}, u32[]{:S(2)}) collective-permute-start(bf16[160,1408]{1,0:T(8,128)(2,1)} %collective-permute-done.4), channel_id=1, source_target_pairs={{0,4},{2,6},{4,0},{6,2},{1,5},{3,7},{5,1},{7,3},{8,12},{10,14},{12... | collective-permute-start | bytes 1351688 | tf_op jit(solution)/shard_map/ppermute | solution.py:317
  73.5 50.1 %collective-permute-start.7 = (bf16[160,1408]{1,0:T(8,128)(2,1)}, bf16[160,1408]{1,0:T(8,128)(2,1)}, u32[]{:S(2)}, u32[]{:S(2)}) collective-permute-start(bf16[160,1408]{1,0:T(8,128)(2,1)} %collective-permute-done.4), channel_id=1, source_target_pairs={{0,6},{2,4},{4,2},{6,0},{1,7},{3,5},{5,3},{7,1},{8,14},{10,12},{12... | collective-permute-start | bytes 1351688 | tf_op jit(solution)/shard_map/ppermute | solution.py:317
  104.5 20.8 %copy-start.1 = (bf16[1024,640]{1,0:T(8,128)(2,1)}, bf16[1024,640]{1,0:T(8,128)(2,1)S(1)}, u32[]{:S(2)}) copy-start(bf16[1024,640]{1,0:T(8,128)(2,1)S(1)} %get-tuple-element.31.gate) | copy-start | bytes 3932164
  104.5 20.8 %copy-start.3 = (bf16[1024,640]{1,0:T(8,128)(2,1)}, bf16[1024,640]{1,0:T(8,128)(2,1)S(1)}, u32[]{:S(2)}) copy-start(bf16[1024,640]{1,0:T(8,128)(2,1)S(1)} %get-tuple-element.32.up) | copy-start | bytes 3932164
  132.3 45.0 %all-to-all-start.2 = ((bf16[8,64,1280]{2,1,0:T(8,128)(2,1)}), bf16[8,64,1280]{2,1,0:T(8,128)(2,1)S(1)}, u32[]{:S(2)}, u32[]{:S(2)}) async-start(bf16[8,64,1280]{2,1,0:T(8,128)(2,1)} %shard_map.103), calls=%async_computation.2 | async-start | bytes 2621440 | tf_op jit(solution)/shard_map/all_to_all | solution.py:342
  142.5 36.1 %collective-permute-start.8 = (bf16[224,640]{1,0:T(8,128)(2,1)}, bf16[224,640]{1,0:T(8,128)(2,1)}, u32[]{:S(2)}, u32[]{:S(2)}) collective-permute-start(bf16[224,640]{1,0:T(8,128)(2,1)} %get-tuple-element.36), channel_id=1, source_target_pairs={{0,32},{16,48},{32,0},{48,16},{1,33},{17,49},{33,1},{49,17},{2,34}... | collective-permute-start | bytes 860168 | tf_op jit(solution)/shard_map/ppermute | solution.py:287
  178.6 24.3 %all-to-all-start.3 = ((bf16[8,64,640]{2,1,0:T(8,128)(2,1)}), bf16[8,64,640]{2,1,0:T(8,128)(2,1)S(1)}, u32[]{:S(2)}, u32[]{:S(2)}) async-start(bf16[8,64,640]{2,1,0:T(8,128)(2,1)} %copy-done), calls=%async_computation.3 | async-start | bytes 1310720 | tf_op jit(solution)/shard_map/all_to_all | solution.py:346
  182.1 17.9 %collective-permute-start.15 = (bf16[224,640]{1,0:T(8,128)(2,1)}, bf16[224,640]{1,0:T(8,128)(2,1)S(1)}, u32[]{:S(2)}, u32[]{:S(2)}) collective-permute-start(bf16[224,640]{1,0:T(8,128)(2,1)} %get-tuple-element.44), channel_id=1, source_target_pairs={{0,16},{16,0},{32,48},{48,32},{1,17},{17,1},{33,49},{49,33},{2,18}... | collective-permute-start | bytes 860168 | tf_op jit(solution)/shard_map/ppermute | solution.py:287
  184.1 18.8 %collective-permute-start.16 = (bf16[224,640]{1,0:T(8,128)(2,1)}, bf16[224,640]{1,0:T(8,128)(2,1)S(1)}, u32[]{:S(2)}, u32[]{:S(2)}) collective-permute-start(bf16[224,640]{1,0:T(8,128)(2,1)} %get-tuple-element.46), channel_id=1, source_target_pairs={{0,48},{16,32},{32,16},{48,0},{1,49},{17,33},{33,17},{49,1},{2,50}... | collective-permute-start | bytes 860168 | tf_op jit(solution)/shard_map/ppermute | solution.py:287
  205.4 24.9 %all-to-all-start.4 = ((bf16[4,320,224]{2,1,0:T(8,128)(2,1)}), bf16[4,320,224]{2,1,0:T(8,128)(2,1)S(1)}, u32[]{:S(2)}, u32[]{:S(2)}) async-start(bf16[4,320,224]{2,1,0:T(8,128)(2,1)} %shard_map.106), calls=%async_computation.4 | async-start | bytes 1310720 | tf_op jit(solution)/shard_map/all_to_all | solution.py:364
  210.8 27.8 %collective-permute-start.10 = (bf16[4,96,224]{2,1,0:T(8,128)(2,1)}, bf16[4,96,224]{2,1,0:T(8,128)(2,1)S(1)}, u32[]{:S(2)}, u32[]{:S(2)}) collective-permute-start(bf16[4,96,224]{2,1,0:T(8,128)(2,1)} %get-tuple-element.40), channel_id=1, source_target_pairs={{0,8},{8,0},{1,9},{9,1},{2,10},{10,2},{3,11},{11,3},{4,12},{12,4},... | collective-permute-start | bytes 516104 | tf_op jit(solution)/shard_map/ppermute | solution.py:246
  213.9 24.7 %collective-permute-start.11 = (bf16[4,96,224]{2,1,0:T(8,128)(2,1)}, bf16[4,96,224]{2,1,0:T(8,128)(2,1)S(1)}, u32[]{:S(2)}, u32[]{:S(2)}) collective-permute-start(bf16[4,96,224]{2,1,0:T(8,128)(2,1)} %get-tuple-element.41), channel_id=1, source_target_pairs={{0,9},{1,8},{8,1},{9,0},{2,11},{3,10},{10,3},{11,2},{4,13},{5,12},... | collective-permute-start | bytes 516104 | tf_op jit(solution)/shard_map/ppermute | solution.py:247
  215.8 22.8 %collective-permute-start.9 = (bf16[4,96,224]{2,1,0:T(8,128)(2,1)}, bf16[4,96,224]{2,1,0:T(8,128)(2,1)S(1)}, u32[]{:S(2)}, u32[]{:S(2)}) collective-permute-start(bf16[4,96,224]{2,1,0:T(8,128)(2,1)} %get-tuple-element.39), channel_id=1, source_target_pairs={{0,1},{1,0},{2,3},{3,2},{4,5},{5,4},{6,7},{7,6},{8,9},{9,8},{10,11... | collective-permute-start | bytes 516104 | tf_op jit(solution)/shard_map/ppermute | solution.py:245
  231.3 19.7 %copy-start.6 = (bf16[96,384]{1,0:T(8,128)(2,1)S(1)}, bf16[96,384]{1,0:T(8,128)(2,1)}, u32[]{:S(2)}) copy-start(bf16[96,384]{1,0:T(8,128)(2,1)} %copy-done.5) | copy-start | bytes 221188
  231.3 19.7 %all-to-all-start.5 = ((bf16[16,24,224]{2,1,0:T(8,128)(2,1)}), bf16[16,24,224]{2,1,0:T(8,128)(2,1)S(1)}, u32[]{:S(2)}, u32[]{:S(2)}) async-start(bf16[16,24,224]{2,1,0:T(8,128)(2,1)} %bitcast.38), calls=%async_computation.5 | async-start | bytes 393216 | tf_op jit(solution)/shard_map/all_to_all | solution.py:371
  238.7 12.5 %collective-permute-start.12 = (bf16[96,224]{1,0:T(8,128)(2,1)S(1)}, bf16[96,224]{1,0:T(8,128)(2,1)S(1)}, u32[]{:S(2)}, u32[]{:S(2)}) collective-permute-start(bf16[96,224]{1,0:T(8,128)(2,1)S(1)} %get-tuple-element.59), channel_id=1, source_target_pairs={{0,16},{16,0},{32,48},{48,32},{1,17},{17,1},{33,49},{49,33},{2,18}... | collective-permute-start | bytes 129032 | tf_op jit(solution)/shard_map/ppermute | solution.py:287
  241.2 10.0 %collective-permute-start.13 = (bf16[96,224]{1,0:T(8,128)(2,1)S(1)}, bf16[96,224]{1,0:T(8,128)(2,1)S(1)}, u32[]{:S(2)}, u32[]{:S(2)}) collective-permute-start(bf16[96,224]{1,0:T(8,128)(2,1)S(1)} %get-tuple-element.61), channel_id=1, source_target_pairs={{0,32},{16,48},{32,0},{48,16},{1,33},{17,49},{33,1},{49,17},{2,34}... | collective-permute-start | bytes 129032 | tf_op jit(solution)/shard_map/ppermute | solution.py:287
  244.8 8.3 %collective-permute-start.14 = (bf16[96,224]{1,0:T(8,128)(2,1)S(1)}, bf16[96,224]{1,0:T(8,128)(2,1)S(1)}, u32[]{:S(2)}, u32[]{:S(2)}) collective-permute-start(bf16[96,224]{1,0:T(8,128)(2,1)S(1)} %get-tuple-element.60), channel_id=1, source_target_pairs={{0,48},{16,32},{32,16},{48,0},{1,49},{17,33},{33,17},{49,1},{2,50}... | collective-permute-start | bytes 129032 | tf_op jit(solution)/shard_map/ppermute | solution.py:287
  (8 other events, 60.6 us)
